TPU v7x, 512 devices: a whole 4x8x8 slice. The times are simulated.
512 devices in a mesh: dp: 64 (over y_lo, x, z), tensor: 8 (over y_hi, core).
Axes of the slice: x: 4, y: 8 (y_hi: 4, y_lo: 2; y = y_hi * 2 + y_lo), z: 8, core: 2. Of those that a mesh axis runs over, the one named last changes fastest.
Arguments:
- log_feats: bfloat16 [22528, 2048], P('dp', 'tensor'), may hold values from -6 to 6
- kpi_feats: bfloat16 [4096, 1152], P('dp', 'tensor'), may hold values from -6 to 6
- log_proj: bfloat16 [2048, 1152], P('tensor'), may hold values from -0.125 to 0.125
- kpi_proj: bfloat16 [1152, 1152], P('tensor'), may hold values from -0.1875 to 0.1875
- log_ids: int32 [22528], P('dp'), may hold values from 0 to 2047
- kpi_ids: int32 [4096], P('dp'), may hold values from 0 to 2047
Outputs:
- grad_log_feats: bfloat16 [22528, 2048], P('dp', 'tensor')
- grad_kpi_proj: float32 [1152, 1152], P('tensor')
Inputs may be any that keep to these rules, and one draw needn't show every extreme that they name: `kpi_ids`: ids of the KPI series, compared with those of the log windows.
All inputs are finite; a program needn't handle non-finite values.
Results may differ from a plain program's by a relative error of at most 0.008.
Values may be sent and summed in bfloat16 or wider, within the bound.
A program may use at most 64 MiB of HBM per device.

v0:
```python
import jax
import jax.numpy as jnp
from jax import lax
from jax.sharding import PartitionSpec as P

SOFTMAX_TEMPER = 32.0
LOGIT_OFFSET_BIAS = -2.0
LOSS_MULTIPLIER = 4096.0
EPSILON = 1e-06


def normalize(vectors):
    inverse = lax.rsqrt(jnp.sum(vectors * vectors, axis=1, keepdims=True) + EPSILON)
    return (vectors * inverse, inverse)


def backward(unit_rows, inverse, upstream):
    inner = jnp.sum(unit_rows * upstream, axis=1, keepdims=True)
    return (inverse * (upstream - unit_rows * inner)).astype(jnp.bfloat16)


def body(log_feats, kpi_feats, log_proj, kpi_proj, log_ids, kpi_ids):
    tensor_count = lax.axis_size("tensor")
    tensor_index = lax.axis_index("tensor")
    rotation_count = lax.axis_size("dp")
    log_window_rows = log_feats.shape[0]
    kpi_rows = kpi_feats.shape[0]
    slice_rows = kpi_rows // tensor_count
    gradient_scale = SOFTMAX_TEMPER * LOSS_MULTIPLIER / (log_window_rows * rotation_count)
    log_part = jnp.dot(log_feats, log_proj, preferred_element_type=jnp.float32)
    kpi_part = jnp.dot(kpi_feats, kpi_proj, preferred_element_type=jnp.float32)
    log_pre = lax.psum(log_part, "tensor")
    kpi_pre = lax.psum_scatter(kpi_part, "tensor", scatter_dimension=0, tiled=True)
    log_unit, log_inv = normalize(log_pre)
    kpi_unit, kpi_inv = normalize(kpi_pre)
    log_emb = log_unit.astype(jnp.bfloat16)
    metric_embedding = kpi_unit.astype(jnp.bfloat16)
    own_ids = lax.dynamic_slice_in_dim(kpi_ids, tensor_index * slice_rows, slice_rows)
    emb_piece = lax.all_gather(metric_embedding, "dp", axis=0, tiled=True)
    id_piece = lax.all_gather(own_ids, "dp", axis=0, tiled=True)
    pair_logits = (
        SOFTMAX_TEMPER
        * jnp.einsum("ne,me->nm", log_emb, emb_piece, preferred_element_type=jnp.float32)
        + LOGIT_OFFSET_BIAS
    )
    pair_sign = jnp.where(log_ids[:, None] == id_piece[None, :], 1.0, -1.0).astype(jnp.float32)
    margin = -pair_sign * pair_logits
    pair_grad = (-gradient_scale * pair_sign * jax.nn.sigmoid(margin)).astype(jnp.bfloat16)
    log_grad = jnp.dot(pair_grad, emb_piece, preferred_element_type=jnp.float32)
    log_grad, pair_grads = (log_grad, pair_grad)
    kpi_grad = lax.psum_scatter(
        jnp.einsum("nm,ne->me", pair_grads, log_emb, preferred_element_type=jnp.float32),
        "dp",
        scatter_dimension=0,
        tiled=True,
    )
    kpi_back = backward(kpi_unit, kpi_inv, kpi_grad)
    log_full = lax.psum(log_grad, "tensor")
    log_back = backward(log_unit, log_inv, log_full)
    kpi_back_all = lax.all_gather(kpi_back, "tensor", axis=0, tiled=True)
    grad_log_feats = jnp.einsum(
        "ne,ke->nk", log_back, log_proj, preferred_element_type=jnp.float32
    ).astype(jnp.bfloat16)
    weight_part = jnp.einsum(
        "mk,me->ke", kpi_feats, kpi_back_all, preferred_element_type=jnp.float32
    )
    grad_kpi_proj = lax.psum(weight_part, "dp")
    return (grad_log_feats, grad_kpi_proj)


def solution(mesh):
    return jax.shard_map(
        body,
        mesh=mesh,
        in_specs=(
            P("dp", "tensor"),
            P("dp", "tensor"),
            P("tensor", None),
            P("tensor", None),
            P("dp"),
            P("dp"),
        ),
        out_specs=(P("dp", "tensor"), P("tensor", None)),
        check_vma=False,
    )
```

profile of v0, /device:TPU:56, one launch (start us, length us, event | category | flops | bytes accessed | tf_op | source)
XLA Modules:
  0.0 1692.5 jit_solution(9982550663501859929)
XLA Ops:
  7.2 0.0 all-reduce.15.cloned.1.call-start
  7.2 2.0 fusion.14
  9.2 2.5 fusion.13
  11.7 0.0 all-reduce.15.cloned.1.call-update
  11.7 0.0 all-gather.2.cloned.1.call-start
  11.8 1.3 dynamic-slice.1
  13.7 87.7 %all-reduce.15.cloned.1.call-done = (f32[64,1152]{1,0:T(8,128)}, f32[352,1152]{1,0:T(8,128)}) async-done(((f32[64,1152]{1,0:T(8,128)}, f32[352,1152]{1,0:T(8,128)}), (f32[64,1152]{1,0:T(8,128)}, f32[352,1152]{1,0:T(8,128)})) %all-reduce.15.cloned.1.call-update) | async-done | bytes 1916944
  101.4 1.0 multiply_reduce_fusion.3
  102.4 1.5 fusion.10
  103.9 0.0 all-gather.2.cloned.1.call-update
  103.9 0.0 all-reduce.13.cloned.1.call-start
  104.0 0.6 fusion.12
  105.2 0.2 dynamic-slice_dynamic-update-slice_fusion
  105.4 24.5 %all-reduce = s32[512]{0:T(512)S(1)} all-reduce(s32[512]{0:T(512)S(1)} %dynamic-slice_dynamic-update-slice_fusion), channel_id=1, replica_groups=mesh['dp'=64,'tensor'=8] {'dp'}, use_global_device_ids=true, to_apply=%add | all-reduce | flops 512 | bytes 4096
  129.9 1.6 multiply_reduce_fusion.1
  131.5 277.0 %all-gather.2.cloned.1.call-done = bf16[512,1152]{1,0:T(8,128)(2,1)} async-done(((bf16[8,1152]{1,0:T(8,128)(2,1)}), bf16[512,1152]{1,0:T(8,128)(2,1)}) %all-gather.2.cloned.1.call-update) | async-done | bytes 1179664 | tf_op jit(solution)/shard_map/all_gather | solution.py:39
  408.5 2.1 fusion.7
  410.7 2.3 fusion.11
  413.0 0.0 all-reduce.9.cloned.1.call-start
  413.1 3.1 fusion.15
  416.2 0.0 all-reduce.11.cloned.1.call-start
  416.9 604.4 %all-reduce.13.cloned.1.call-done = f32[512,1152]{1,0:T(8,128)} async-done(((f32[512,1152]{1,0:T(8,128)}), f32[512,1152]{1,0:T(8,128)}) %all-reduce.13.cloned.1.call-update) | async-done | bytes 2359312
  1021.3 1.0 multiply_reduce_fusion.2
  1022.2 0.9 multiply_convert_fusion.3
  1023.1 15.1 all_gather.11
  1038.2 1.1 convolution_bitcast_fusion
  1039.4 63.9 %all-reduce.9.cloned.1.call-done = f32[352,1152]{1,0:T(8,128)} async-done(((f32[352,1152]{1,0:T(8,128)}), f32[352,1152]{1,0:T(8,128)}) %all-reduce.9.cloned.1.call-update) | async-done | bytes 1622032 | tf_op jit(solution)/shard_map/psum | solution.py:58
  1103.3 1.9 multiply_reduce_fusion
  1105.2 0.1 copy-done.2
  1105.2 1.1 convolution_convert_fusion
  1106.4 577.6 %all-reduce.11.cloned.1.call-done = f32[144,1152]{1,0:T(8,128)} async-done(((f32[144,1152]{1,0:T(8,128)}), f32[144,1152]{1,0:T(8,128)}) %all-reduce.11.cloned.1.call-update) | async-done | bytes 663568 | tf_op jit(solution)/shard_map/psum | solution.py:67
  1684.0 2.0 copy.14
  (19 shorter events, 0.1 us)
Async XLA Ops:
  7.2 2.0 copy-start
  7.2 94.2 %all-reduce.15.cloned.1.call-start = ((), (), s32[]{:S(2)}) async-start(), calls=%async_computation.4 | async-start | bytes 3833856
  11.7 92.3 %copy-start.4 = (u32[512]{0:T(512)S(1)}, u32[512]{0:T(512)}, u32[]{:S(2)}) copy-start(u32[512]{0:T(512)} %constant.30) | copy-start | bytes 6148
  11.7 93.5 %copy-start.5 = (s32[64]{0:T(128)S(1)}, s32[64]{0:T(128)}, u32[]{:S(2)}) copy-start(s32[64]{0:T(128)} %param.11) | copy-start | bytes 772
  11.7 396.9 %copy-start.6 = (s32[352]{0:T(512)S(1)}, s32[352]{0:T(512)}, u32[]{:S(2)}) copy-start(s32[352]{0:T(512)} %param.10) | copy-start | bytes 4228
  11.7 396.8 %all-gather.2.cloned.1.call-start = ((), (), s32[]{:S(2)}) async-start(), calls=%async_computation | async-start | bytes 1198080 | tf_op jit(solution)/shard_map/all_gather | solution.py:39
  101.4 307.1 %copy-start.1 = (f32[352,1152]{1,0:T(8,128)S(1)}, f32[352,1152]{1,0:T(8,128)}, u32[]{:S(2)}) copy-start(f32[352,1152]{1,0:T(8,128)} %get-tuple-element.3) | copy-start | bytes 4866052
  103.9 917.4 %all-reduce.13.cloned.1.call-start = ((), (), s32[]{:S(2)}) async-start(), calls=%async_computation.3 | async-start | bytes 4718592
  413.0 690.3 %all-reduce.9.cloned.1.call-start = ((), (), s32[]{:S(2)}) async-start(), calls=%async_computation.1 | async-start | bytes 3244032 | tf_op jit(solution)/shard_map/psum | solution.py:58
  416.1 622.1 %copy-start.3 = (bf16[64,144]{1,0:T(8,128)(2,1)S(1)}, bf16[64,144]{1,0:T(8,128)(2,1)}, u32[]{:S(2)}) copy-start(bf16[64,144]{1,0:T(8,128)(2,1)} %param.7) | copy-start | bytes 55300
  416.2 1267.8 %all-reduce.11.cloned.1.call-start = ((), (), s32[]{:S(2)}) async-start(), calls=%async_computation.2 | async-start | bytes 1327104 | tf_op jit(solution)/shard_map/psum | solution.py:67
  1103.3 1.9 copy-start.2
Sparse Core Ops, SparseCore 0:
  11.8 89.5 all-reduce.14
  104.3 304.2 all-gather.1
  413.1 608.1 all-reduce.12
  1024.1 79.1 all-reduce.8
  1106.6 577.2 all-reduce.10
where the time goes:
time: 1690 us
  waiting for transfers between devices  1610 us (95%)
  blocking collectives  39.6 us (2%)
    unnamed x7, waiting for transfers between devices  692 us
    psum x1, waiting for transfers between devices, body(): grad_kpi_proj = lax.psum(weight_part, 'dp')  578 us
    all_gather x1, waiting for transfers between devices, body(): emb_piece = lax.all_gather(metric_embedding, 'dp', axis=0, tiled=True)  277 us
    psum x1, waiting for transfers between devices, body(): log_full = lax.psum(log_grad, 'tensor')  63.9 us
  transfers between devices with their start and end apart: 5, of which 5 were waited for; matrix products, arithmetic and copies ran while one was open for 1% of the time, Pallas kernels for 0%

commit v1 on v0

v1 whole, which is shorter than its diff:
```python
import jax
import jax.numpy as jnp
from jax import lax
from jax.experimental import pallas as pl
from jax.experimental.pallas import tpu as pltpu
from jax.sharding import PartitionSpec as P

TEMPER = 32.0
BIAS = -2.0
LOSS = 4096.0
EPS = 1e-06
MESH = pl.DeviceIdType.MESH
BF = jnp.bfloat16
F32 = jnp.float32

NY, NX, NZ, NH = 2, 4, 8, 4
LOG = 352
HALF = LOG // 2
BLK = 48
HP = NH * BLK
E = 1152
ID = 128
EK = E + ID
GROUP = 64
OWN = 8
COUNT = NY * NX * NZ * OWN
SCALE = TEMPER * LOSS / (LOG * NY * NX * NZ)
WROWS = 176
NSEM = 128


def dot(a, b):
    return jnp.dot(a, b, preferred_element_type=F32)


def dot_t(a, b):
    return lax.dot_general(a, b, (((1,), (1,)), ((), ())), preferred_element_type=F32)


def mod(a, n):
    return lax.rem(a, jnp.int32(n))


def digits(ids):
    high = jnp.floor(ids * (1.0 / 256.0))
    rest = ids - 256.0 * high
    middle = jnp.floor(rest * (1.0 / 16.0))
    return high, middle, rest - 16.0 * middle


def on_lanes(values, rows):
    lane = lax.broadcasted_iota(jnp.int32, (rows, ID), 1)
    out = jnp.zeros((rows, ID), F32)
    for at, value in enumerate(values):
        out = jnp.where(lane == at, value, out)
    return out


def pair_gradient(inner, apart):
    sign = jnp.where(apart < 0.5, 1.0, -1.0).astype(F32)
    margin = -sign * (TEMPER * inner + BIAS)
    return (-SCALE * sign * jax.nn.sigmoid(margin)).astype(BF)


def kernel(
    lf, kf, lp, kp, lid, kid, out_g, out_w,
    lsend, lrecv, lacc, lysend, lyrecv, lall, lunit, lext,
    kacc, ksend, krecv, kysend, kyrecv, kmsg, kgot, kall, kunit,
    pg, kg, lg,
    gsend, grecv, gysend, gyrecv, back,
    zrs, zrr, zls, zlr, xrs, xrr, xls, xlr, mid, midsend, midrecv, mid16, ymsg, ygot,
    kback, wbuf, wzr, wx, wy, wall,
    ssem, rsem,
):
    d = lax.axis_index("dp")
    t = lax.axis_index("tensor")
    y = lax.div(d, jnp.int32(NX * NZ))
    x = mod(lax.div(d, jnp.int32(NZ)), NX)
    z = mod(d, NZ)
    h = lax.div(t, jnp.int32(2))
    c = mod(t, 2)
    used = [0]

    def place(y=y, x=x, z=z, h=h, c=c):
        return {"dp": (y * NX + x) * NZ + z, "tensor": h * 2 + c}

    def sem():
        used[0] += 1
        return used[0] - 1

    def copy(at, src, dst, device):
        return pltpu.make_async_remote_copy(
            src_ref=src, dst_ref=dst, send_sem=ssem.at[at], recv_sem=rsem.at[at],
            device_id=device, device_id_type=MESH,
        )

    def rows(start, size, unit):
        return pl.ds(pl.multiple_of(start, unit), size)

    partner = place(c=1 - c)
    other_y = place(y=1 - y)
    hpeer = [place(h=mod(h + r, NH)) for r in range(NH)]
    hfrom = [mod(h + NH - r, NH) for r in range(NH)]
    xpeer = [place(x=mod(x + r, NX)) for r in range(NX)]
    xfrom = [mod(x + NX - r, NX) for r in range(NX)]
    zpeer = [place(z=mod(z + r, NZ)) for r in range(NZ)]
    zfrom = [mod(z + NZ - r, NZ) for r in range(NZ)]

    barrier = pltpu.get_barrier_semaphore()
    peers = [partner, other_y] + hpeer[1:] + xpeer[1:] + zpeer[1:]
    for device in peers:
        pl.semaphore_signal(barrier, inc=1, device_id=device, device_id_type=MESH)

    pending = []

    kacc[...] = dot(kf[...], kp[...])
    ksend[...] = kacc[rows(32 * (1 - c), 32, 32), :]
    lsend[:HALF, :] = dot(lf[rows(HALF * (1 - c), HALF, 16), :], lp[...]).astype(BF)
    lsend[HALF:, :] = jnp.zeros((HP - HALF, E), BF)

    pl.semaphore_wait(barrier, len(peers))
    k_core = copy(sem(), ksend, krecv, partner)
    k_core.start()
    l_core = copy(sem(), lsend, lrecv, partner)
    l_core.start()
    pending += [k_core, l_core]

    lacc[:HALF, :] = dot(lf[rows(HALF * c, HALF, 16), :], lp[...])
    lacc[HALF:, :] = jnp.zeros((HP - HALF, E), F32)

    k_core.wait_recv()
    waits = []
    for r in (2, 1, 3):
        to = mod(h + r, NH)
        kysend[r - 1] = kacc[rows(32 * c + OWN * to, OWN, OWN), :] + krecv[rows(OWN * to, OWN, OWN), :]
        go = copy(sem(), kysend.at[r - 1], kyrecv.at[r - 1], hpeer[r])
        go.start()
        waits.append(go)
    pending += waits

    l_core.wait_recv()
    l_waits = []
    for r in (2, 1, 3):
        at = rows(BLK * mod(h + r, NH), BLK, 16)
        lysend[r - 1] = (lacc[at, :] + lrecv[at, :].astype(F32)).astype(BF)
        go = copy(sem(), lysend.at[r - 1], lyrecv.at[r - 1], hpeer[r])
        go.start()
        l_waits.append(go)
    pending += l_waits

    row_ids = lax.broadcasted_iota(jnp.int32, (OWN, GROUP), 0) + (32 * c + OWN * h)
    col_ids = lax.broadcasted_iota(jnp.int32, (OWN, GROUP), 1)
    own_id = jnp.sum(jnp.where(row_ids == col_ids, kid[...].astype(F32), 0.0), axis=1, keepdims=True)
    one = jnp.ones_like(own_id)
    own_digit = digits(own_id)
    own_ext = on_lanes(list(own_digit) + [g * g for g in own_digit] + [one] * 3, OWN)
    kmsg[:, E:] = own_ext

    at = lax.broadcasted_iota(jnp.int32, (2 * HP, LOG), 0)
    upper = at >= HP
    inside = jnp.where(upper, at - HP, at)
    at = jnp.where(inside < HALF, jnp.where(upper, inside + HALF, inside), -1)
    col = lax.broadcasted_iota(jnp.int32, (2 * HP, LOG), 1)
    log_id = jnp.sum(jnp.where(at == col, lid[...].astype(F32), 0.0), axis=1, keepdims=True)
    one = jnp.ones_like(log_id)
    log_digit = digits(log_id)
    lext[...] = on_lanes([-2.0 * g for g in log_digit] + [one] * 3 + [g * g for g in log_digit], 2 * HP).astype(BF)

    own = kacc[rows(32 * c + OWN * h, OWN, OWN), :] + krecv[rows(OWN * h, OWN, OWN), :]
    for go in waits:
        go.wait_recv()
    own = own + kyrecv[0] + kyrecv[1] + kyrecv[2]
    k_inv = lax.rsqrt(jnp.sum(own * own, axis=1, keepdims=True) + EPS)
    unit = own * k_inv
    kunit[...] = unit
    kmsg[:, :E] = unit.astype(BF).astype(F32)
    y_copy = copy(sem(), kmsg, kgot, other_y)
    y_copy.start()
    pending.append(y_copy)
    y_copy.wait_recv()

    both = jnp.concatenate([jnp.where(y == 0, kmsg[...], kgot[...]), jnp.where(y == 0, kgot[...], kmsg[...])], axis=0)
    both = both.astype(BF)

    at_zx = [lambda zz, xx: 64 * zz + 16 * xx, lambda zz, xx: 128 * xx + 16 * zz]
    first = {0: [], 1: []}
    second = {0: [], 1: []}

    def direct_gather(core, peer, position):
        base = rows(at_zx[core](z, x), 16, 16)
        kall[base, :] = both
        for r in range(1, len(peer)):
            go = copy(first[core][r - 1], kall.at[base, :], kall.at[base, :], peer[r])
            go.start()

    def direct_gather_recv(core, come):
        for r in range(1, len(come)):
            base = rows(at_zx[core](z, come[r]) if core == 0 else at_zx[core](come[r], x), 16, 16)
            copy(first[core][r - 1], kall.at[base, :], kall.at[base, :], partner).wait_recv()

    def direct_gather_sent(core, peer):
        base = rows(at_zx[core](z, x), 16, 16)
        for r in range(1, len(peer)):
            copy(first[core][r - 1], kall.at[base, :], kall.at[base, :], peer[r]).wait_send()

    first[0] = [sem() for _ in range(NX - 1)]
    first[1] = [sem() for _ in range(NZ - 1)]

    @pl.when(c == 0)
    def _():
        direct_gather(0, xpeer, x)

    @pl.when(c == 1)
    def _():
        direct_gather(1, zpeer, z)

    def ring_steps(n, size):
        half = n // 2
        steps = []
        for s in range(half):
            whole = s < half - 1
            steps.append((s, (0, size) if whole else (0, size // 2), (0, size) if whole else (size // 2, size // 2)))
        return steps

    class Ring:
        def __init__(self, n, at, size, peer):
            self.n, self.at, self.size, self.peer = n, at, size, peer
            self.steps = ring_steps(n, size)
            self.right = [sem() for _ in self.steps]
            self.left = [sem() for _ in self.steps]

        def block(self, which, part):
            return kall.at[rows(self.size * mod(which + self.n, self.n) + part[0], part[1], 16), :]

        def start(self, s):
            _, right, left = self.steps[s]
            ref = self.block(self.at - s, right)
            copy(self.right[s], ref, ref, self.peer[1]).start()
            ref = self.block(self.at + s, left)
            copy(self.left[s], ref, ref, self.peer[self.n - 1]).start()

        def recv(self, s):
            _, right, left = self.steps[s]
            ref = self.block(self.at - 1 - s, right)
            copy(self.right[s], ref, ref, self.peer[1]).wait_recv()
            ref = self.block(self.at + 1 + s, left)
            copy(self.left[s], ref, ref, self.peer[self.n - 1]).wait_recv()

        def sent(self):
            for s, right, left in self.steps:
                ref = self.block(self.at - s, right)
                copy(self.right[s], ref, ref, self.peer[1]).wait_send()
                ref = self.block(self.at + s, left)
                copy(self.left[s], ref, ref, self.peer[self.n - 1]).wait_send()

    ring = [Ring(NZ, z, 64, zpeer), Ring(NX, x, 128, xpeer)]

    @pl.when(c == 0)
    def _():
        direct_gather_recv(0, xfrom)
        ring[0].start(0)

    @pl.when(c == 1)
    def _():
        direct_gather_recv(1, zfrom)
        ring[1].start(0)

    mine = rows(BLK * h, BLK, 16)
    for go in l_waits:
        go.wait_recv()
    row = lacc[mine, :] + lrecv[mine, :].astype(F32)
    for r in range(NH - 1):
        row = row + lyrecv[r].astype(F32)
    l_inv = lax.rsqrt(jnp.sum(row * row, axis=1, keepdims=True) + EPS)
    row = row * l_inv
    lunit[...] = row

    def spread(buffer, value):
        mine = rows(HP * c + BLK * h, BLK, 16)
        buffer[mine, :] = value
        ref = buffer.at[mine, :]
        along = []
        across = []
        for r in (2, 1, 3):
            go = copy(sem(), ref, ref, hpeer[r])
            go.start()
            come = buffer.at[rows(HP * c + BLK * hfrom[r], BLK, 16), :]
            along.append((r, go, come))
        go = copy(sem(), ref, ref, partner)
        go.start()
        across.append((0, go))
        pending.extend([g for _, g, _ in along] + [go])
        return along, across

    def spread_end(buffer, along, across):
        for r, go, come in along[1:] + along[:1]:
            go.wait_recv()
            on = copy(sem(), come, come, partner)
            on.start()
            across.append((r, on))
            pending.append(on)
        for r, on in across:
            ref = buffer.at[rows(HP * (1 - c) + BLK * hfrom[r], BLK, 16), :]
            on.wait_recv()

    l_along, l_across = spread(lall, row.astype(BF))

    @pl.when(c == 0)
    def _():
        for s in range(1, NZ // 2):
            ring[0].recv(s - 1)
            ring[0].start(s)

    @pl.when(c == 1)
    def _():
        for s in range(1, NX // 2):
            ring[1].recv(s - 1)
            ring[1].start(s)

    spread_end(lall, l_along, l_across)

    @pl.when(c == 0)
    def _():
        ring[0].recv(NZ // 2 - 1)

    @pl.when(c == 1)
    def _():
        ring[1].recv(NX // 2 - 1)

    def kpi_side(i, carry):
        at = rows(i * 128, 128, 128)
        inner = dot_t(kall[at, :E], lall[...])
        apart = dot_t(kall[at, E:], lext[...])
        kg[at, :] = dot(pair_gradient(inner, apart), lall[...])
        return carry

    lax.fori_loop(0, COUNT // 128, kpi_side, 0)

    class Sum:
        def __init__(self, n, at, size, peer, bufs):
            self.n, self.at, self.size, self.peer = n, at, size, peer
            self.rs, self.rr, self.ls, self.lr = bufs
            self.right = [sem() for _ in range(n // 2)]
            self.left = [sem() for _ in range(n // 2)]

        def part(self, which, start, size):
            return kg[rows(self.size * mod(which + self.n, self.n) + start, size, 16), :]

        def copies(self, s):
            half = self.size // 2
            right, left = (pl.ds(0, half), pl.ds(half, half)) if s == 0 else (pl.ds(0, self.size),) * 2
            return (
                copy(self.right[s], self.rs.at[s, right], self.rr.at[s, right], self.peer[1]),
                copy(self.left[s], self.ls.at[s, left], self.lr.at[s, left], self.peer[self.n - 1]),
            )

        def start(self, s):
            n, half = self.n, self.size // 2
            right, left = self.copies(s)
            if s == 0:
                self.rs[0, :half] = self.part(self.at + n // 2, 0, half).astype(BF)
                self.ls[0, half:] = self.part(self.at + n // 2, half, half).astype(BF)
            elif s == 1:
                to = self.at + n // 2 - 1
                self.rs[1, :half] = (self.part(to, 0, half) + self.rr[0, :half].astype(F32)).astype(BF)
                self.rs[1, half:] = self.part(to, half, half).astype(BF)
                right.start()
                to = self.at - n // 2 + 1
                self.ls[1, :half] = self.part(to, 0, half).astype(BF)
                self.ls[1, half:] = (self.part(to, half, half) + self.lr[0, half:].astype(F32)).astype(BF)
                left.start()
                return
            else:
                to = self.at + n // 2 - s
                self.rs[s] = (self.part(to, 0, self.size) + self.rr[s - 1].astype(F32)).astype(BF)
                right.start()
                to = self.at - n // 2 + s
                self.ls[s] = (self.part(to, 0, self.size) + self.lr[s - 1].astype(F32)).astype(BF)
                left.start()
                return
            right.start()
            left.start()

        def recv(self, s):
            for go in self.copies(s):
                go.wait_recv()

        def result(self):
            last = self.n // 2 - 1
            return self.part(self.at, 0, self.size) + self.rr[last].astype(F32) + self.lr[last].astype(F32)

        def sent(self):
            for s in range(self.n // 2):
                for go in self.copies(s):
                    go.wait_send()

    sums = [Sum(NZ, z, 64, zpeer, (zrs, zrr, zls, zlr)), Sum(NX, x, 128, xpeer, (xrs, xrr, xls, xlr))]
    mid_sem = [[sem() for _ in range(NX - 1)], [sem() for _ in range(NZ - 1)]]

    @pl.when(c == 0)
    def _():
        sums[0].start(0)

    @pl.when(c == 1)
    def _():
        sums[1].start(0)

    def log_pairs(i, carry):
        at = rows(i * 128, 128, 128)
        inner = dot_t(lall[...], kall[at, :E])
        apart = dot_t(lext[...], kall[at, E:])
        pg[:, at] = pair_gradient(inner, apart)
        return carry

    lax.fori_loop(0, COUNT // 128, log_pairs, 0)
    gsend[...] = dot(pg[rows(HP * (1 - c), HP, 16), :], kall[:, :E]).astype(BF)
    g_core = copy(sem(), gsend, grecv, partner)
    g_core.start()
    pending.append(g_core)

    @pl.when(c == 0)
    def _():
        sums[0].recv(0)
        sums[0].start(1)

    @pl.when(c == 1)
    def _():
        sums[1].recv(0)
        sums[1].start(1)

    lg[...] = dot(pg[rows(HP * c, HP, 16), :], kall[:, :E])

    g_core.wait_recv()
    g_waits = []
    for r in (2, 1, 3):
        at = rows(BLK * mod(h + r, NH), BLK, 16)
        gysend[r - 1] = (lg[at, :] + grecv[at, :].astype(F32)).astype(BF)
        go = copy(sem(), gysend.at[r - 1], gyrecv.at[r - 1], hpeer[r])
        go.start()
        g_waits.append(go)
    pending += g_waits

    def middle(core, peer, go_first):
        for r in range(1, len(peer)):
            if go_first:
                to = mod((x if core == 0 else z) + r, len(peer))
                midsend[r - 1] = mid[rows(16 * to, 16, 16), :].astype(BF)
            go = copy(mid_sem[core][r - 1], midsend.at[r - 1], midrecv.at[r - 1], peer[r])
            if go_first:
                go.start()
            else:
                go.wait_send()

    def middle_end(core, peer):
        total = mid[rows(16 * (x if core == 0 else z), 16, 16), :]
        for r in range(1, len(peer)):
            copy(mid_sem[core][r - 1], midsend.at[r - 1], midrecv.at[r - 1], peer[r]).wait_recv()
            total = total + midrecv[r - 1].astype(F32)
        mid16[...] = total

    @pl.when(c == 0)
    def _():
        for s in range(1, NZ // 2):
            sums[0].recv(s)
            if s < NZ // 2 - 1:
                sums[0].start(s + 1)
        mid[:64, :] = sums[0].result()
        middle(0, xpeer, True)
        middle_end(0, xpeer)

    @pl.when(c == 1)
    def _():
        for s in range(1, NX // 2):
            sums[1].recv(s)
            if s < NX // 2 - 1:
                sums[1].start(s + 1)
        mid[...] = sums[1].result()
        middle(1, zpeer, True)
        middle_end(1, zpeer)

    ymsg[...] = mid16[rows(OWN * (1 - y), OWN, OWN), :]
    y_back = copy(sem(), ymsg, ygot, other_y)
    y_back.start()
    pending.append(y_back)

    y_back.wait_recv()
    total = mid16[rows(OWN * y, OWN, OWN), :] + ygot[...]
    unit = kunit[...]
    inner = jnp.sum(unit * total, axis=1, keepdims=True)
    mine8 = rows(32 * c + OWN * h, OWN, OWN)
    kback[mine8, :] = (k_inv * (total - unit * inner)).astype(BF).astype(F32)
    kb_waits = []
    for r in (2, 1, 3):
        go = copy(sem(), kback.at[mine8, :], kback.at[mine8, :], hpeer[r])
        go.start()
        kb_waits.append(go)
    pending += kb_waits

    for go in g_waits:
        go.wait_recv()
    row = lg[mine, :] + grecv[mine, :].astype(F32)
    for r in range(NH - 1):
        row = row + gyrecv[r].astype(F32)
    unit = lunit[...]
    inner = jnp.sum(unit * row, axis=1, keepdims=True)
    b_along, b_across = spread(back, (l_inv * (row - unit * inner)).astype(BF))

    for go in kb_waits:
        go.wait_recv()
    half = kback.at[rows(32 * c, 32, 32), :]
    kb_core = copy(sem(), half, half, partner)
    kb_core.start()
    pending.append(kb_core)
    kb_core.wait_recv()

    part = lax.dot_general(
        kf[...], kback[...].astype(BF), (((0,), (0,)), ((), ())), preferred_element_type=F32
    ).astype(BF)
    tall = part.shape[0]
    for j in range(E // 128):
        wbuf[tall * j : tall * (j + 1), :] = part[:, 128 * j : 128 * (j + 1)]
    wbuf[tall * (E // 128) :, :] = jnp.zeros((NZ * WROWS - tall * (E // 128), 128), BF)
    w_waits = []
    for r in (4, 3, 5, 2, 6, 1, 7):
        go = copy(sem(), wbuf.at[rows(WROWS * mod(z + r, NZ), WROWS, 16), :], wzr.at[r - 1], zpeer[r])
        go.start()
        w_waits.append(go)
    pending += w_waits

    spread_end(back, b_along, b_across)
    for i in range(2):
        out_g[HALF * i : HALF * (i + 1), :] = dot_t(back[HP * i : HP * i + HALF, :], lp[...]).astype(BF)

    total = wbuf[rows(WROWS * z, WROWS, 16), :].astype(F32)
    for go in w_waits:
        go.wait_recv()
    for r in range(NZ - 1):
        total = total + wzr[r].astype(F32)
    wx[x] = total.astype(BF)
    x_waits = []
    for r in (2, 1, 3):
        go = copy(sem(), wx.at[x], wx.at[x], xpeer[r])
        go.start()
        x_waits.append(go)
    pending += x_waits
    for go in x_waits:
        go.wait_recv()
    total = wx[0].astype(F32)
    for i in range(1, NX):
        total = total + wx[i].astype(F32)
    wy[y] = total.astype(BF)
    go = copy(sem(), wy.at[y], wy.at[y], other_y)
    go.start()
    pending.append(go)
    go.wait_recv()
    share = rows(WROWS * z, WROWS, 16)
    wall[share, :] = (wy[0].astype(F32) + wy[1].astype(F32)).astype(BF)
    w_waits = []
    for r in (4, 3, 5, 2, 6, 1, 7):
        go = copy(sem(), wall.at[share, :], wall.at[share, :], zpeer[r])
        go.start()
        w_waits.append(go)
    pending += w_waits
    for go in w_waits:
        go.wait_recv()
    for j in range(E // 128):
        out_w[:, 128 * j : 128 * (j + 1)] = wall[tall * j : tall * (j + 1), :].astype(F32)

    for go in pending:
        go.wait_send()

    @pl.when(c == 0)
    def _():
        direct_gather_sent(0, xpeer)
        ring[0].sent()
        sums[0].sent()
        middle(0, xpeer, False)

    @pl.when(c == 1)
    def _():
        direct_gather_sent(1, zpeer)
        ring[1].sent()
        sums[1].sent()
        middle(1, zpeer, False)

    assert used[0] <= NSEM


def body(log_feats, kpi_feats, log_proj, kpi_proj, log_ids, kpi_ids):
    v = pltpu.VMEM
    scratch = [
        v((HP, E), BF), v((HP, E), BF), v((HP, E), F32), v((3, BLK, E), BF), v((3, BLK, E), BF),
        v((2 * HP, E), BF), v((BLK, E), F32), v((2 * HP, ID), BF),
        v((GROUP, E), F32), v((32, E), F32), v((32, E), F32), v((3, OWN, E), F32), v((3, OWN, E), F32),
        v((OWN, EK), F32), v((OWN, EK), F32), v((COUNT, EK), BF), v((OWN, E), F32),
        v((2 * HP, COUNT), BF), v((COUNT, E), F32), v((HP, E), F32),
        v((HP, E), BF), v((HP, E), BF), v((3, BLK, E), BF), v((3, BLK, E), BF), v((2 * HP, E), BF),
        v((4, 64, E), BF), v((4, 64, E), BF), v((4, 64, E), BF), v((4, 64, E), BF),
        v((2, 128, E), BF), v((2, 128, E), BF), v((2, 128, E), BF), v((2, 128, E), BF),
        v((128, E), F32), v((7, 16, E), BF), v((7, 16, E), BF), v((16, E), F32), v((OWN, E), F32), v((OWN, E), F32),
        v((GROUP, E), F32), v((NZ * WROWS, 128), BF), v((NZ - 1, WROWS, 128), BF), v((NX, WROWS, 128), BF),
        v((NY, WROWS, 128), BF), v((NZ * WROWS, 128), BF),
        pltpu.SemaphoreType.DMA((NSEM,)), pltpu.SemaphoreType.DMA((NSEM,)),
    ]
    return pl.pallas_call(
        kernel,
        out_shape=(
            jax.ShapeDtypeStruct(log_feats.shape, BF),
            jax.ShapeDtypeStruct(kpi_proj.shape, F32),
        ),
        in_specs=[pl.BlockSpec(memory_space=v)] * 6,
        out_specs=(pl.BlockSpec(memory_space=v),) * 2,
        scratch_shapes=scratch,
        compiler_params=pltpu.CompilerParams(
            collective_id=0, has_side_effects=True, vmem_limit_bytes=48 * 1024 * 1024
        ),
    )(log_feats, kpi_feats, log_proj, kpi_proj, log_ids.reshape(1, -1), kpi_ids.reshape(1, -1))


def solution(mesh):
    return jax.shard_map(
        body,
        mesh=mesh,
        in_specs=(
            P("dp", "tensor"),
            P("dp", "tensor"),
            P("tensor", None),
            P("tensor", None),
            P("dp"),
            P("dp"),
        ),
        out_specs=(P("dp", "tensor"), P("tensor", None)),
        check_vma=False,
    )
```

time: 1690 us -> 126 us (0.07)
  the two profiles are of different devices: /device:TPU:56 before, /device:TPU:1 now
where the time goes in v1:
time: 126 us; the launch traced here: 125 us
  Pallas kernels  119 us (94%)
  local copies, waits for them, and re-layouts  5.92 us (5%)
    pallas_call x1, Pallas kernels, body(): pl.pallas_call(kernel, out_shape=(jax.ShapeDtypeStruct(log_feats.shape, B...  119 us
    unnamed x12, local copies, waits for them, and re-layouts  5.23 us

profile of v1, /device:TPU:1, one launch (start us, length us, event | category | flops | bytes accessed | tf_op | source)
XLA Modules:
  0.0 125.2 jit_solution(7569025414764805621)
XLA Ops:
  0.6 0.0 copy-start.4
  0.6 0.7 reshape.10.lid
  1.3 0.0 copy-done.4
  1.3 0.0 copy-start
  1.3 1.1 copy-done
  2.4 0.0 copy-start.1
  2.4 1.0 copy-done.1
  3.4 0.0 copy-start.2
  3.4 0.9 copy-done.2
  4.3 0.0 copy-start.3
  4.3 0.8 copy-done.3
  5.1 118.6 %shard_map.77 = (bf16[352,256]{1,0:T(8,128)(2,1)S(1)}, f32[144,1152]{1,0:T(8,128)S(1)}) custom-call(bf16[352,256]{1,0:T(8,128)(2,1)S(1)} %copy-done.2, bf16[64,144]{1,0:T(8,128)(2,1)S(1)} %copy-done.3, bf16[256,1152]{1,0:T(8,128)(2,1)S(1)} %copy-done, bf16[144,1152]{1,0:T(8,128)(2,1)S(1)} %copy-done.1, s32[1,352]{1,0:T(1,128)S(1)} %reshape.10.lid, ...), custom_call_target="tpu_custom_call" | custom-call | tf_op jit(solution)/shard_map/pallas_call | solution.py:605
  123.6 0.7 copy.10
  124.3 0.8 copy.11
Async XLA Ops:
  0.6 0.7 copy-start.4
  1.3 1.1 copy-start
  2.4 1.0 copy-start.1
  3.4 0.9 copy-start.2
  4.3 0.8 copy-start.3

commit v2 on v0

v2 whole, which is shorter than its diff:
```python
import jax
import jax.numpy as jnp
from jax import lax
from jax.experimental import pallas as pl
from jax.experimental.pallas import tpu as pltpu
from jax.sharding import PartitionSpec as P

TEMPER = 32.0
BIAS = -2.0
LOSS = 4096.0
EPS = 1e-06
MESH = pl.DeviceIdType.MESH
BF = jnp.bfloat16
F32 = jnp.float32

NY, NX, NZ, NH = 2, 4, 8, 4
LOG = 352
HALF = LOG // 2
BLK = 48
HP = NH * BLK
E = 1152
ID = 128
EK = E + ID
GROUP = 64
OWN = 8
COUNT = NY * NX * NZ * OWN
SCALE = TEMPER * LOSS / (LOG * NY * NX * NZ)
PK = EK // 2
CUT = 32
WZ, WX = 176, 336
XS, ZS = (2, 1, 3), (4, 3, 5, 2, 6, 1, 7)
NSEM = 160


def dot(a, b):
    return jnp.dot(a, b, preferred_element_type=F32)


def dot_t(a, b):
    return lax.dot_general(a, b, (((1,), (1,)), ((), ())), preferred_element_type=F32)


def mod(a, n):
    return lax.rem(a, jnp.int32(n))


def digits(ids):
    high = jnp.floor(ids * (1.0 / 256.0))
    rest = ids - 256.0 * high
    middle = jnp.floor(rest * (1.0 / 16.0))
    return high, middle, rest - 16.0 * middle


def on_lanes(values, rows):
    lane = lax.broadcasted_iota(jnp.int32, (rows, ID), 1)
    out = jnp.zeros((rows, ID), F32)
    for at, value in enumerate(values):
        out = jnp.where(lane == at, value, out)
    return out


def pair_gradient(inner, apart):
    sign = jnp.where(apart < 0.5, 1.0, -1.0).astype(F32)
    margin = -sign * (TEMPER * inner + BIAS)
    return (-SCALE * sign * jax.nn.sigmoid(margin)).astype(BF)


def kernel(
    lf_h, kf_h, lp_h, kp_h, lid_h, kid_h, out_g, out_w,
    lf, kf, lp, kp, lid, kid, og, ow,
    lsend, lrecv, lacc, lrs, lrr, lls, llr, lall, lunit, lext,
    kacc, ksend, krecv, kysend, kyrecv, kmsg, kgot, kall, kunit,
    pg, kg, lg, gsend, grecv, grs, grr, gls, glr, back,
    zrs, zrr, zls, zlr, xrs, xrr, xls, xlr, mid, midsend, midrecv, mid16, ymsg, ygot,
    kback, wbuf, wzr, wxr, wx, wy, wxs, wxzr, wys, wxz, wall,
    ssem, rsem, lsem,
):
    d = lax.axis_index("dp")
    t = lax.axis_index("tensor")
    y = lax.div(d, jnp.int32(NX * NZ))
    x = mod(lax.div(d, jnp.int32(NZ)), NX)
    z = mod(d, NZ)
    h = lax.div(t, jnp.int32(2))
    c = mod(t, 2)

    def place(y=y, x=x, z=z, h=h, c=c):
        return {"dp": (y * NX + x) * NZ + z, "tensor": h * 2 + c}

    def rows(start, size, unit=16):
        return pl.ds(pl.multiple_of(start, unit), size)

    started = []

    class Send:
        def __init__(self, src, dst, to, land=None, core=None):
            self.src, self.dst, self.to, self.core = src, dst, to, core
            self.land = land or dst
            self.at = len(started)
            self.open, self.begun = True, False
            started.append(self)
            assert self.at < NSEM

        def copy(self, src, dst):
            return pltpu.make_async_remote_copy(
                src_ref=src(), dst_ref=dst(), send_sem=ssem.at[self.at], recv_sem=rsem.at[self.at],
                device_id=self.to, device_id_type=MESH,
            )

        def start(self):
            self.begun = True
            self.copy(self.src, self.dst).start()

        def recv(self):
            self.open = False
            self.copy(self.land, self.land).wait_recv()

        def sent(self):
            self.copy(self.src, self.dst).wait_send()

    def finish():
        for core in (None, 0, 1):

            def ends(core=core):
                for go in started:
                    if go.core == core and go.begun:
                        if go.open:
                            go.recv()
                        go.sent()

            if core is None:
                ends()
            else:
                pl.when(c == core)(ends)

    inputs = [
        pltpu.make_async_copy(a, b, lsem.at[i])
        for i, (a, b) in enumerate(((kf_h, kf), (kp_h, kp), (lf_h, lf), (lp_h, lp), (kid_h, kid), (lid_h, lid)))
    ]
    for go in inputs:
        go.start()

    partner = place(c=1 - c)
    other_y = place(y=1 - y)
    hpeer = [place(h=mod(h + r, NH)) for r in range(NH)]
    hfrom = [mod(h + NH - r, NH) for r in range(NH)]
    xpeer = [place(x=mod(x + r, NX)) for r in range(NX)]
    xfrom = [mod(x + NX - r, NX) for r in range(NX)]
    zpeer = [place(z=mod(z + r, NZ)) for r in range(NZ)]
    zfrom = [mod(z + NZ - r, NZ) for r in range(NZ)]

    barrier = pltpu.get_barrier_semaphore()
    peers = [partner, other_y] + hpeer[1:] + xpeer[1:] + zpeer[1:]
    for device in peers:
        pl.semaphore_signal(barrier, inc=1, device_id=device, device_id_type=MESH)

    def on_core(run):
        for core in (0, 1):
            pl.when(c == core)(lambda core=core: run(core))

    def packed(v):
        if v.shape[1] < EK:
            v = jnp.concatenate([v, jnp.zeros((OWN, EK - v.shape[1]), F32)], axis=1)
        return jnp.concatenate([v[:, :PK], v[:, PK:]], axis=0).astype(BF)

    def unpacked(v):
        v = v.astype(F32)
        return jnp.concatenate([v[:OWN], v[OWN:]], axis=1)

    class Gather:
        def __init__(self, n, at, size, split, right, left, block, sign=1, core=None):
            self.n, self.go = n, []
            whole = [((0, size), (0, size))] * (n // 2 - 1)
            for s, (a, b) in enumerate(whole + [((0, split), (split, size - split))]):
                there, here = block(at - sign * s, a), block(at - sign * (s + 1), a)
                one = Send(there, there, right, here, core)
                there, here = block(at + sign * s, b), block(at + sign * (s + 1), b)
                self.go.append((one, Send(there, there, left, here, core)))

        def start(self, s):
            for go in self.go[s]:
                go.start()

        def recv(self, s):
            for go in self.go[s]:
                go.recv()

    class Sum:
        def __init__(self, n, at, size, split, right, left, part, bufs, sign=1, core=None):
            self.n, self.at, self.size, self.split, self.part, self.sign = n, at, size, split, part, sign
            self.rs, self.rr, self.ls, self.lr = bufs
            self.go = []
            for s in range(n // 2):
                parts = ((0, split), (split, size - split)) if s == 0 else ((0, size), (0, size))
                pair = []
                for p, send, come, to in ((parts[0], self.rs, self.rr, right), (parts[1], self.ls, self.lr, left)):
                    src = lambda s=s, p=p, send=send: send.at[s, pl.ds(*p)]
                    dst = lambda s=s, p=p, come=come: come.at[s, pl.ds(*p)]
                    pair.append(Send(src, dst, to, core=core))
                self.go.append(pair)

        def start(self, s):
            k, size, part = self.split, self.size, self.part
            away = self.n // 2 - s
            to = self.at + self.sign * away
            if s == 0:
                self.rs[0, :k] = part(to, 0, k).astype(BF)
                self.go[0][0].start()
                self.ls[0, k:] = part(to, k, size - k).astype(BF)
                self.go[0][1].start()
                return
            if s == 1:
                self.rs[1, :k] = (part(to, 0, k) + self.rr[0, :k].astype(F32)).astype(BF)
                self.rs[1, k:] = part(to, k, size - k).astype(BF)
            else:
                self.rs[s] = (part(to, 0, size) + self.rr[s - 1].astype(F32)).astype(BF)
            self.go[s][0].start()
            to = self.at - self.sign * away
            if s == 1:
                self.ls[1, :k] = part(to, 0, k).astype(BF)
                self.ls[1, k:] = (part(to, k, size - k) + self.lr[0, k:].astype(F32)).astype(BF)
            else:
                self.ls[s] = (part(to, 0, size) + self.lr[s - 1].astype(F32)).astype(BF)
            self.go[s][1].start()

        def recv(self, s):
            for go in self.go[s]:
                go.recv()

        def result(self):
            last = self.n // 2 - 1
            return self.part(self.at, 0, self.size) + self.rr[last].astype(F32) + self.lr[last].astype(F32)

    turn = 1 - 2 * c
    h_right = place(h=mod(h + turn + NH, NH))
    h_left = place(h=mod(h - turn + NH, NH))

    def h_sum(own, come, bufs):
        def part(which, start, size):
            at = rows(BLK * mod(which + NH, NH) + start, size)
            return own[at, :] + come[at, :].astype(F32)

        return Sum(NH, h, BLK, CUT, h_right, h_left, part, bufs, turn)

    class Spread:
        def __init__(self, buffer):
            self.buffer = buffer

            def at_core(core):
                def block(hh, part=(0, BLK)):
                    return lambda: buffer.at[rows(HP * core + BLK * mod(hh + NH, NH) + part[0], part[1]), :]

                return block

            mine, other = at_core(c), at_core(1 - c)
            self.along = Gather(NH, h, BLK, CUT, h_right, h_left, mine, turn)
            self.across = {r: Send(mine(h - r), mine(h - r), partner, other(h - r)) for r in (0, 1, 3, 2)}

        def start(self, value):
            self.buffer[rows(HP * c + BLK * h, BLK), :] = value
            self.along.start(0)
            self.across[0].start()

        def step(self):
            self.along.recv(0)
            self.along.start(1)
            self.across[1].start()
            self.across[3].start()

        def last(self):
            self.along.recv(1)
            self.across[2].start()

        def end(self):
            for go in self.across.values():
                go.recv()

    inputs[0].wait()
    inputs[1].wait()
    kacc[...] = dot(kf[...], kp[...])
    ksend[...] = kacc[rows(32 * (1 - c), 32, 32), :].astype(BF)
    inputs[2].wait()
    inputs[3].wait()
    lsend[:HALF, :] = dot(lf[rows(HALF * (1 - c), HALF), :], lp[...]).astype(BF)
    lsend[HALF:, :] = jnp.zeros((HP - HALF, E), BF)
    inputs[4].wait()
    inputs[5].wait()

    pl.semaphore_wait(barrier, len(peers))
    k_core = Send(lambda: ksend, lambda: krecv, partner)
    k_core.start()
    l_core = Send(lambda: lsend, lambda: lrecv, partner)
    l_core.start()

    lacc[:HALF, :] = dot(lf[rows(HALF * c, HALF), :], lp[...])
    lacc[HALF:, :] = jnp.zeros((HP - HALF, E), F32)

    def k_part(to):
        return kacc[rows(32 * c + OWN * to, OWN, OWN), :]

    k_core.recv()
    kacc[rows(32 * c, 32, 32), :] += krecv[...].astype(F32)
    k_waits = []
    for r in (2, 1, 3):
        kysend[r - 1] = packed(k_part(mod(h + r, NH)))
        go = Send(lambda r=r: kysend.at[r - 1], lambda r=r: kyrecv.at[r - 1], hpeer[r])
        go.start()
        k_waits.append(go)

    l_sum = h_sum(lacc, lrecv, (lrs, lrr, lls, llr))
    l_core.recv()
    l_sum.start(0)

    row_ids = lax.broadcasted_iota(jnp.int32, (OWN, GROUP), 0) + (32 * c + OWN * h)
    col_ids = lax.broadcasted_iota(jnp.int32, (OWN, GROUP), 1)
    own_id = jnp.sum(jnp.where(row_ids == col_ids, kid[...].astype(F32), 0.0), axis=1, keepdims=True)
    one = jnp.ones_like(own_id)
    own_digit = digits(own_id)
    k_ext = on_lanes(list(own_digit) + [g * g for g in own_digit] + [one] * 3, OWN)

    l_sum.recv(0)
    l_sum.start(1)

    own = k_part(h)
    for go in k_waits:
        go.recv()
    for r in range(NH - 1):
        own = own + unpacked(kyrecv[r])[:, :E]
    k_inv = lax.rsqrt(jnp.sum(own * own, axis=1, keepdims=True) + EPS)
    unit = own * k_inv
    kunit[...] = unit
    kmsg[...] = packed(jnp.concatenate([unit, k_ext], axis=1))
    y_copy = Send(lambda: kmsg, lambda: kgot, other_y)
    y_copy.start()

    at = lax.broadcasted_iota(jnp.int32, (2 * HP, LOG), 0)
    upper = at >= HP
    inside = jnp.where(upper, at - HP, at)
    at = jnp.where(inside < HALF, jnp.where(upper, inside + HALF, inside), -1)
    col = lax.broadcasted_iota(jnp.int32, (2 * HP, LOG), 1)
    log_id = jnp.sum(jnp.where(at == col, lid[...].astype(F32), 0.0), axis=1, keepdims=True)
    one = jnp.ones_like(log_id)
    log_digit = digits(log_id)
    lext[...] = on_lanes([-2.0 * g for g in log_digit] + [one] * 3 + [g * g for g in log_digit], 2 * HP).astype(BF)

    y_copy.recv()
    sent, got = unpacked(kmsg[...]), unpacked(kgot[...])
    both = jnp.concatenate([jnp.where(y == 0, sent, got), jnp.where(y == 0, got, sent)], axis=0).astype(BF)

    def block0(zz, xx):
        return kall.at[rows(64 * zz + 16 * xx, 16), :]

    def block1(zz, xx):
        return kall.at[rows(128 * xx + 16 * zz, 16), :]

    own0 = lambda: block0(z, x)
    own1 = lambda: block1(z, x)
    first = [
        [Send(own0, own0, xpeer[r], lambda r=r: block0(z, xfrom[r]), 0) for r in XS],
        [Send(own1, own1, zpeer[r], lambda r=r: block1(zfrom[r], x), 1) for r in ZS],
    ]

    def k_block(n, size):
        return lambda which, part: lambda: kall.at[rows(size * mod(which + n, n) + part[0], part[1]), :]

    ring = [
        Gather(NZ, z, 64, 32, zpeer[1], zpeer[NZ - 1], k_block(NZ, 64), core=0),
        Gather(NX, x, 128, 64, xpeer[1], xpeer[NX - 1], k_block(NX, 128), core=1),
    ]

    @on_core
    def _(core):
        base = rows(64 * z + 16 * x, 16) if core == 0 else rows(128 * x + 16 * z, 16)
        kall[base, :] = both
        for go in first[core]:
            go.start()

    @on_core
    def _(core):
        for go in first[core]:
            go.recv()
        ring[core].start(0)


    l_sum.recv(1)
    row = l_sum.result()
    l_inv = lax.rsqrt(jnp.sum(row * row, axis=1, keepdims=True) + EPS)
    row = row * l_inv
    lunit[...] = row
    l_spread = Spread(lall)
    l_spread.start(row.astype(BF))

    @on_core
    def _(core):
        for s in range(1, ring[core].n // 2):
            ring[core].recv(s - 1)
            ring[core].start(s)

    l_spread.step()
    l_spread.last()

    @on_core
    def _(core):
        ring[core].recv(ring[core].n // 2 - 1)

    l_spread.end()

    lead = jnp.where(c == 0, lax.div(mod(z + NZ // 2, NZ), jnp.int32(2)), mod(x + NX // 2, NX))

    def kpi_side(i, carry):
        at = rows(mod(lead + i, 4) * 128, 128, 128)
        inner = dot_t(kall[at, :E], lall[...])
        apart = dot_t(kall[at, E:], lext[...])
        kg[at, :] = dot(pair_gradient(inner, apart), lall[...])
        return carry

    def k_part_of(n, size):
        return lambda which, start, count: kg[rows(size * mod(which + n, n) + start, count), :]

    sums = [
        Sum(NZ, z, 64, 32, zpeer[1], zpeer[NZ - 1], k_part_of(NZ, 64), (zrs, zrr, zls, zlr), core=0),
        Sum(NX, x, 128, 64, xpeer[1], xpeer[NX - 1], k_part_of(NX, 128), (xrs, xrr, xls, xlr), core=1),
    ]

    def step(s):
        @on_core
        def _(core):
            if s < sums[core].n // 2:
                if s > 0:
                    sums[core].recv(s - 1)
                sums[core].start(s)

    kpi_side(0, 0)
    step(0)
    lax.fori_loop(1, COUNT // 128, kpi_side, 0)
    step(1)

    def log_pairs(i, carry):
        at = rows(i * 256, 256, 256)
        inner = dot_t(lall[...], kall[at, :E])
        apart = dot_t(lext[...], kall[at, E:])
        pg[:, at] = pair_gradient(inner, apart)
        return carry

    lax.fori_loop(0, COUNT // 256, log_pairs, 0)
    gsend[...] = dot(pg[rows(HP * (1 - c), HP), :], kall[:, :E]).astype(BF)
    g_core = Send(lambda: gsend, lambda: grecv, partner)
    g_core.start()
    step(2)
    lg[...] = dot(pg[rows(HP * c, HP), :], kall[:, :E])

    g_sum = h_sum(lg, grecv, (grs, grr, gls, glr))
    g_core.recv()
    g_sum.start(0)
    step(3)

    middle = [
        [Send(lambda r=r: midsend.at[r - 1], lambda r=r: midrecv.at[r - 1], xpeer[r], core=0) for r in XS],
        [Send(lambda r=r: midsend.at[r - 1], lambda r=r: midrecv.at[r - 1], zpeer[r], core=1) for r in ZS],
    ]

    g_sum.recv(0)
    g_sum.start(1)

    @on_core
    def _(core):
        at, order = ((x, XS), (z, ZS))[core]
        n = len(order) + 1
        sums[core].recv(sums[core].n // 2 - 1)
        mid[: 16 * n, :] = sums[core].result()
        for r, go in zip(order, middle[core]):
            midsend[r - 1] = mid[rows(16 * mod(at + r, n), 16), :].astype(BF)
            go.start()
        total = mid[rows(16 * at, 16), :]
        for go in middle[core]:
            go.recv()
        for r in range(n - 1):
            total = total + midrecv[r].astype(F32)
        mid16[...] = total

    ymsg[...] = packed(mid16[rows(OWN * (1 - y), OWN, OWN), :])
    y_back = Send(lambda: ymsg, lambda: ygot, other_y)
    y_back.start()
    y_back.recv()
    total = mid16[rows(OWN * y, OWN, OWN), :] + unpacked(ygot[...])[:, :E]
    unit = kunit[...]
    inner = jnp.sum(unit * total, axis=1, keepdims=True)
    kback[c * NH + h] = packed(k_inv * (total - unit * inner))

    def kblock(hh):
        return lambda: kback.at[c * NH + hh]

    kb_waits = [Send(kblock(h), kblock(h), hpeer[r], kblock(hfrom[r])) for r in (2, 1, 3)]
    for go in kb_waits:
        go.start()

    g_sum.recv(1)
    row = g_sum.result()
    unit = lunit[...]
    inner = jnp.sum(unit * row, axis=1, keepdims=True)
    row = (l_inv * (row - unit * inner)).astype(BF)

    def khalf(core):
        return lambda: kback.at[pl.ds(core * NH, NH)]

    for go in kb_waits:
        go.recv()
    kb_core = Send(khalf(c), khalf(c), partner, khalf(1 - c))
    kb_core.start()
    b_spread = Spread(back)
    b_spread.start(row)
    kb_core.recv()

    rows_back = jnp.concatenate([unpacked(kback[i])[:, :E] for i in range(2 * NH)], axis=0).astype(BF)
    part = lax.dot_general(kf[...], rows_back, (((0,), (0,)), ((), ())), preferred_element_type=F32).astype(BF)
    tall = part.shape[0]
    for j in range(E // 128):
        wbuf[tall * j : tall * (j + 1), :] = part[:, 128 * j : 128 * (j + 1)]
    wbuf[tall * (E // 128) :, :] = jnp.zeros((NZ * WZ - tall * (E // 128), 128), BF)

    def cut_of(ref, size, at):
        return lambda: ref.at[rows(size * at, size), :]

    def slot(ref, at):
        return lambda: ref.at[at]

    w_first = [
        [Send(cut_of(wbuf, WZ, mod(z + r, NZ)), slot(wzr, r - 1), zpeer[r], core=0) for r in ZS],
        [Send(cut_of(wbuf, WX, mod(x + r, NX)), slot(wxr, r - 1), xpeer[r], core=1) for r in XS],
    ]
    w_second = [
        [Send(slot(wx, x), slot(wx, x), xpeer[r], slot(wx, xfrom[r]), 0) for r in XS],
        [Send(cut_of(wxs, BLK, mod(z + r, NZ)), slot(wxzr, r - 1), zpeer[r], core=1) for r in ZS],
    ]
    w_pair = [
        [Send(slot(wy, y), slot(wy, y), other_y, slot(wy, 1 - y), 0)],
        [Send(slot(wys, y), slot(wys, y), other_y, slot(wys, 1 - y), 1)],
    ]
    w_third = [
        [],
        [Send(cut_of(wxz, BLK, z), cut_of(wxz, BLK, z), zpeer[r], cut_of(wxz, BLK, zfrom[r]), 1) for r in ZS],
    ]
    w_last = [
        [Send(cut_of(wall, WZ, z), cut_of(wall, WZ, z), zpeer[r], cut_of(wall, WZ, zfrom[r]), 0) for r in ZS],
        [Send(cut_of(wall, WX, x), cut_of(wall, WX, x), xpeer[r], cut_of(wall, WX, xfrom[r]), 1) for r in XS],
    ]

    def begin(copies):
        for go in copies:
            go.start()

    def arrive(copies):
        for go in copies:
            go.recv()

    @on_core
    def _(core):
        begin(w_first[core])

    b_spread.step()

    @on_core
    def _(core):
        if core == 0:
            total = wbuf[rows(WZ * z, WZ), :].astype(F32)
            arrive(w_first[0])
            for r in range(NZ - 1):
                total = total + wzr[r].astype(F32)
            wx[x] = total.astype(BF)
        else:
            total = wbuf[rows(WX * x, WX), :].astype(F32)
            arrive(w_first[1])
            for r in range(NX - 1):
                total = total + wxr[r].astype(F32)
            wxs[:WX, :] = total.astype(BF)
            wxs[WX:, :] = jnp.zeros((NZ * BLK - WX, 128), BF)
        begin(w_second[core])

    b_spread.last()

    @on_core
    def _(core):
        arrive(w_second[core])
        if core == 0:
            total = wx[0].astype(F32)
            for i in range(1, NX):
                total = total + wx[i].astype(F32)
            wy[y] = total.astype(BF)
        else:
            total = wxs[rows(BLK * z, BLK), :].astype(F32)
            for r in range(NZ - 1):
                total = total + wxzr[r].astype(F32)
            wys[y] = total.astype(BF)
        begin(w_pair[core])


    @on_core
    def _(core):
        arrive(w_pair[core])
        if core == 0:
            wall[rows(WZ * z, WZ), :] = (wy[0].astype(F32) + wy[1].astype(F32)).astype(BF)
            begin(w_last[0])
        else:
            wxz[rows(BLK * z, BLK), :] = (wys[0].astype(F32) + wys[1].astype(F32)).astype(BF)
            begin(w_third[1])
            arrive(w_third[1])
            wall[rows(WX * x, WX), :] = wxz[:WX, :]
            begin(w_last[1])

    b_spread.end()
    for i in range(2):
        og[HALF * i : HALF * (i + 1), :] = dot_t(back[HP * i : HP * i + HALF, :], lp[...]).astype(BF)
    g_out = pltpu.make_async_copy(og, out_g, lsem.at[6])
    g_out.start()

    @on_core
    def _(core):
        arrive(w_last[core])

    for j in range(E // 128):
        ow[:, 128 * j : 128 * (j + 1)] = wall[tall * j : tall * (j + 1), :].astype(F32)
    w_out = pltpu.make_async_copy(ow, out_w, lsem.at[7])
    w_out.start()
    finish()
    g_out.wait()
    w_out.wait()


def body(log_feats, kpi_feats, log_proj, kpi_proj, log_ids, kpi_ids):
    v = pltpu.VMEM
    inputs = (log_feats, kpi_feats, log_proj, kpi_proj, log_ids.reshape(1, -1), kpi_ids.reshape(1, -1))
    outs = (jax.ShapeDtypeStruct(log_feats.shape, BF), jax.ShapeDtypeStruct(kpi_proj.shape, F32))
    scratch = [v(a.shape, a.dtype) for a in inputs + outs] + [
        v((HP, E), BF), v((HP, E), BF), v((HP, E), F32), *[v((2, BLK, E), BF)] * 4,
        v((2 * HP, E), BF), v((BLK, E), F32), v((2 * HP, ID), BF),
        v((GROUP, E), F32), v((32, E), BF), v((32, E), BF), v((3, 16, PK), BF), v((3, 16, PK), BF),
        v((16, PK), BF), v((16, PK), BF), v((COUNT, EK), BF), v((OWN, E), F32),
        v((2 * HP, COUNT), BF), v((COUNT, E), F32), v((HP, E), F32),
        v((HP, E), BF), v((HP, E), BF), *[v((2, BLK, E), BF)] * 4, v((2 * HP, E), BF),
        *[v((4, 64, E), BF)] * 4, *[v((2, 128, E), BF)] * 4,
        v((128, E), F32), v((7, 16, E), BF), v((7, 16, E), BF), v((16, E), F32), v((16, PK), BF), v((16, PK), BF),
        v((2 * NH, 16, PK), BF), v((NZ * WZ, 128), BF), v((NZ - 1, WZ, 128), BF), v((NX - 1, WX, 128), BF),
        v((NX, WZ, 128), BF), v((NY, WZ, 128), BF), v((NZ * BLK, 128), BF), v((NZ - 1, BLK, 128), BF),
        v((NY, BLK, 128), BF), v((NZ * BLK, 128), BF), v((NZ * WZ, 128), BF),
        pltpu.SemaphoreType.DMA((NSEM,)), pltpu.SemaphoreType.DMA((NSEM,)),
        pltpu.SemaphoreType.DMA((8,)),
    ]
    return pl.pallas_call(
        kernel,
        out_shape=outs,
        in_specs=[pl.BlockSpec(memory_space=pltpu.HBM)] * 6,
        out_specs=(pl.BlockSpec(memory_space=pltpu.HBM),) * 2,
        scratch_shapes=scratch,
        compiler_params=pltpu.CompilerParams(
            collective_id=0, has_side_effects=True, vmem_limit_bytes=62 * 1024 * 1024
        ),
    )(*inputs)


def solution(mesh):
    return jax.shard_map(
        body,
        mesh=mesh,
        in_specs=(
            P("dp", "tensor"),
            P("dp", "tensor"),
            P("tensor", None),
            P("tensor", None),
            P("dp"),
            P("dp"),
        ),
        out_specs=(P("dp", "tensor"), P("tensor", None)),
        check_vma=False,
    )
```

time: 1690 us -> 115 us (0.07)
  the two profiles are of different devices: /device:TPU:56 before, /device:TPU:1 now
where the time goes in v2:
time: 115 us
  Pallas kernels  110 us (96%)
  local copies, waits for them, and re-layouts  4.82 us (4%)
    pallas_call x1, Pallas kernels, body(): pl.pallas_call(kernel, out_shape=outs, in_specs=[pl.BlockSpec(memory_spac...  110 us
    unnamed x2, local copies, waits for them, and re-layouts  3.58 us

profile of v2, /device:TPU:1, one launch (start us, length us, event | category | flops | bytes accessed | tf_op | source)
XLA Modules:
  0.0 115.0 jit_solution(9610223742629327327)
XLA Ops:
  0.6 1.2 %reshape.10.lid_h = s32[1,352]{1,0:T(1,128)} reshape(s32[352]{0:T(512)} %param.10) | data formatting | bytes 2816 | tf_op jit(solution)/shard_map/reshape | solution.py:630
  1.9 109.6 %shard_map.77 = (bf16[352,256]{1,0:T(8,128)(2,1)}, f32[144,1152]{1,0:T(8,128)}) custom-call(bf16[352,256]{1,0:T(8,128)(2,1)} %lf_h.1, bf16[64,144]{1,0:T(8,128)(2,1)} %kf_h.1, bf16[256,1152]{1,0:T(8,128)(2,1)} %lp_h.1, bf16[144,1152]{1,0:T(8,128)(2,1)} %kp_h.1, s32[1,352]{1,0:T(1,128)} %reshape.10.lid_h, s32[1,64]{1,0:T(1,128)} %bitcast.1), custom_call_target="tpu_custom_call" | custom-call | tf_op jit(solution)/shard_map/pallas_call | solution.py:647
  111.5 1.6 %copy.10 = bf16[352,256]{1,0:T(8,128)(2,1)} copy(bf16[352,256]{1,0:T(8,128)(2,1)} %get-tuple-element.4) | data formatting | bytes 360448
  113.1 2.0 %copy.11 = f32[144,1152]{1,0:T(8,128)} copy(f32[144,1152]{1,0:T(8,128)} %get-tuple-element.5) | data formatting | bytes 1327104

commit v3 on v2

--- a/solution.py
+++ b/solution.py
@@ -67,11 +67,11 @@
 
 def kernel(
     lf_h, kf_h, lp_h, kp_h, lid_h, kid_h, out_g, out_w,
-    lf, kf, lp, kp, lid, kid, og, ow,
+    lf, kf, lp, kp, lid, kid, og,
     lsend, lrecv, lacc, lrs, lrr, lls, llr, lall, lunit, lext,
-    kacc, ksend, krecv, kysend, kyrecv, kmsg, kgot, kall, kunit,
+    kacc, ksend, krecv, kysend, kyrecv, kfo, kf2, kido, kall, kunit,
     pg, kg, lg, gsend, grecv, grs, grr, gls, glr, back,
-    zrs, zrr, zls, zlr, xrs, xrr, xls, xlr, mid, midsend, midrecv, mid16, ymsg, ygot,
+    zrs, zrr, zls, zlr, xrs, xrr, xls, xlr, mid, midsend, midrecv, mid16,
     kback, wbuf, wzr, wxr, wx, wy, wxs, wxzr, wys, wxz, wall,
     ssem, rsem, lsem,
 ):
@@ -140,7 +140,7 @@
         go.start()
 
     partner = place(c=1 - c)
-    other_y = place(y=1 - y)
+    ypeer = {(r, f): place(h=mod(h + r, NH), y=y if f == 0 else 1 - y) for r in range(NH) for f in (0, 1)}
     hpeer = [place(h=mod(h + r, NH)) for r in range(NH)]
     hfrom = [mod(h + NH - r, NH) for r in range(NH)]
     xpeer = [place(x=mod(x + r, NX)) for r in range(NX)]
@@ -149,7 +149,7 @@
     zfrom = [mod(z + NZ - r, NZ) for r in range(NZ)]
 
     barrier = pltpu.get_barrier_semaphore()
-    peers = [partner, other_y] + hpeer[1:] + xpeer[1:] + zpeer[1:]
+    peers = [partner] + [ypeer[k] for k in ypeer if k != (0, 0)] + xpeer[1:] + zpeer[1:]
     for device in peers:
         pl.semaphore_signal(barrier, inc=1, device_id=device, device_id_type=MESH)
 
@@ -169,61 +169,58 @@
     class Gather:
         def __init__(self, n, at, size, split, right, left, block, sign=1, core=None):
             self.n, self.go = n, []
-            whole = [((0, size), (0, size))] * (n // 2 - 1)
-            for s, (a, b) in enumerate(whole + [((0, split), (split, size - split))]):
-                there, here = block(at - sign * s, a), block(at - sign * (s + 1), a)
-                one = Send(there, there, right, here, core)
-                there, here = block(at + sign * s, b), block(at + sign * (s + 1), b)
-                self.go.append((one, Send(there, there, left, here, core)))
-
-        def start(self, s):
-            for go in self.go[s]:
+            low, high = (0, split), (split, size - split)
+            ways = [(right, -sign, low), (left, sign, high), (right, -sign, high), (left, sign, low)]
+            for s in range(n // 2):
+                step = []
+                for to, way, part in ways if s < n // 2 - 1 else ways[:2]:
+                    there, here = block(at + way * s, part), block(at + way * (s + 1), part)
+                    step.append(Send(there, there, to, here, core))
+                self.go.append(step)
+
+        def step(self, s):
+            for i, go in enumerate(self.go[s]):
+                if s > 0:
+                    self.go[s - 1][i].recv()
                 go.start()
 
         def recv(self, s):
             for go in self.go[s]:
-                go.recv()
+                if go.open:
+                    go.recv()
+
+        def end(self):
+            for s in range(self.n // 2):
+                self.recv(s)
 
     class Sum:
         def __init__(self, n, at, size, split, right, left, part, bufs, sign=1, core=None):
-            self.n, self.at, self.size, self.split, self.part, self.sign = n, at, size, split, part, sign
+            self.n, self.at, self.size, self.part = n, at, size, part
             self.rs, self.rr, self.ls, self.lr = bufs
+            low, high = (0, split), (split, size - split)
+            r, l = (right, sign, self.rs, self.rr), (left, -sign, self.ls, self.lr)
+            self.ways = [(*r, low), (*l, high), (*r, high), (*l, low)]
             self.go = []
             for s in range(n // 2):
-                parts = ((0, split), (split, size - split)) if s == 0 else ((0, size), (0, size))
-                pair = []
-                for p, send, come, to in ((parts[0], self.rs, self.rr, right), (parts[1], self.ls, self.lr, left)):
+                step = []
+                for to, _, send, come, p in self.ways[:2] if s == 0 else self.ways:
                     src = lambda s=s, p=p, send=send: send.at[s, pl.ds(*p)]
                     dst = lambda s=s, p=p, come=come: come.at[s, pl.ds(*p)]
-                    pair.append(Send(src, dst, to, core=core))
-                self.go.append(pair)
-
-        def start(self, s):
-            k, size, part = self.split, self.size, self.part
-            away = self.n // 2 - s
-            to = self.at + self.sign * away
-            if s == 0:
-                self.rs[0, :k] = part(to, 0, k).astype(BF)
-                self.go[0][0].start()
-                self.ls[0, k:] = part(to, k, size - k).astype(BF)
-                self.go[0][1].start()
-                return
-            if s == 1:
-                self.rs[1, :k] = (part(to, 0, k) + self.rr[0, :k].astype(F32)).astype(BF)
-                self.rs[1, k:] = part(to, k, size - k).astype(BF)
-            else:
-                self.rs[s] = (part(to, 0, size) + self.rr[s - 1].astype(F32)).astype(BF)
-            self.go[s][0].start()
-            to = self.at - self.sign * away
-            if s == 1:
-                self.ls[1, :k] = part(to, 0, k).astype(BF)
-                self.ls[1, k:] = (part(to, k, size - k) + self.lr[0, k:].astype(F32)).astype(BF)
-            else:
-                self.ls[s] = (part(to, 0, size) + self.lr[s - 1].astype(F32)).astype(BF)
-            self.go[s][1].start()
-
-        def recv(self, s):
-            for go in self.go[s]:
+                    step.append(Send(src, dst, to, core=core))
+                self.go.append(step)
+
+        def step(self, s):
+            for i in (0, 1) if s == 0 else (2, 3, 0, 1):
+                _, way, send, come, p = self.ways[i]
+                value = self.part(self.at + way * (self.n // 2 - s), *p)
+                if s > 1 or (s == 1 and i < 2):
+                    self.go[s - 1][i].recv()
+                    value = value + come[s - 1, pl.ds(*p), :].astype(F32)
+                send[s, pl.ds(*p), :] = value.astype(BF)
+                self.go[s][i].start()
+
+        def end(self):
+            for go in self.go[-1]:
                 go.recv()
 
         def result(self):
@@ -257,12 +254,12 @@
 
         def start(self, value):
             self.buffer[rows(HP * c + BLK * h, BLK), :] = value
-            self.along.start(0)
+            self.along.step(0)
             self.across[0].start()
 
         def step(self):
+            self.along.step(1)
             self.along.recv(0)
-            self.along.start(1)
             self.across[1].start()
             self.across[3].start()
 
@@ -294,57 +291,66 @@
     lacc[:HALF, :] = dot(lf[rows(HALF * c, HALF), :], lp[...])
     lacc[HALF:, :] = jnp.zeros((HP - HALF, E), F32)
 
-    def k_part(to):
-        return kacc[rows(32 * c + OWN * to, OWN, OWN), :]
+    f_copy = Send(lambda: kf, lambda: kfo, ypeer[0, 1])
+    f_copy.start()
+    i_copy = Send(lambda: kid, lambda: kido, ypeer[0, 1])
+    i_copy.start()
 
     k_core.recv()
     kacc[rows(32 * c, 32, 32), :] += krecv[...].astype(F32)
     k_waits = []
-    for r in (2, 1, 3):
-        kysend[r - 1] = packed(k_part(mod(h + r, NH)))
-        go = Send(lambda r=r: kysend.at[r - 1], lambda r=r: kyrecv.at[r - 1], hpeer[r])
-        go.start()
-        k_waits.append(go)
+    for r in (2, 1, 3, 0):
+        kysend[r] = packed(kacc[rows(32 * c + OWN * mod(h + r, NH), OWN, OWN), :])
+        for f in (0, 1):
+            if (r, f) != (0, 0):
+                go = Send(lambda r=r: kysend.at[r], lambda r=r, f=f: kyrecv.at[f, r], ypeer[r, f])
+                go.start()
+                k_waits.append(go)
 
     l_sum = h_sum(lacc, lrecv, (lrs, lrr, lls, llr))
     l_core.recv()
-    l_sum.start(0)
+    l_sum.step(0)
+
+    i_copy.recv()
+    f_copy.recv()
+
+    def by_group(own, other):
+        return jnp.concatenate([jnp.where(y == 0, own, other), jnp.where(y == 0, other, own)], axis=0)
 
     row_ids = lax.broadcasted_iota(jnp.int32, (OWN, GROUP), 0) + (32 * c + OWN * h)
     col_ids = lax.broadcasted_iota(jnp.int32, (OWN, GROUP), 1)
-    own_id = jnp.sum(jnp.where(row_ids == col_ids, kid[...].astype(F32), 0.0), axis=1, keepdims=True)
-    one = jnp.ones_like(own_id)
-    own_digit = digits(own_id)
-    k_ext = on_lanes(list(own_digit) + [g * g for g in own_digit] + [one] * 3, OWN)
-
-    l_sum.recv(0)
-    l_sum.start(1)
-
-    own = k_part(h)
-    for go in k_waits:
-        go.recv()
-    for r in range(NH - 1):
-        own = own + unpacked(kyrecv[r])[:, :E]
-    k_inv = lax.rsqrt(jnp.sum(own * own, axis=1, keepdims=True) + EPS)
-    unit = own * k_inv
-    kunit[...] = unit
-    kmsg[...] = packed(jnp.concatenate([unit, k_ext], axis=1))
-    y_copy = Send(lambda: kmsg, lambda: kgot, other_y)
-    y_copy.start()
+
+    def id_column(ref):
+        return jnp.sum(jnp.where(row_ids == col_ids, ref[...].astype(F32), 0.0), axis=1, keepdims=True)
+
+    k_id = by_group(id_column(kid), id_column(kido))
+    one = jnp.ones_like(k_id)
+    k_digit = digits(k_id)
+    k_ext = on_lanes(list(k_digit) + [g * g for g in k_digit] + [one] * 3, 2 * OWN)
 
     at = lax.broadcasted_iota(jnp.int32, (2 * HP, LOG), 0)
     upper = at >= HP
     inside = jnp.where(upper, at - HP, at)
     at = jnp.where(inside < HALF, jnp.where(upper, inside + HALF, inside), -1)
     col = lax.broadcasted_iota(jnp.int32, (2 * HP, LOG), 1)
-    log_id = jnp.sum(jnp.where(at == col, lid[...].astype(F32), 0.0), axis=1, keepdims=True)
+    log_id = jnp.sum(jnp.where(at == col, lid[...].reshape(1, LOG).astype(F32), 0.0), axis=1, keepdims=True)
     one = jnp.ones_like(log_id)
     log_digit = digits(log_id)
     lext[...] = on_lanes([-2.0 * g for g in log_digit] + [one] * 3 + [g * g for g in log_digit], 2 * HP).astype(BF)
 
-    y_copy.recv()
-    sent, got = unpacked(kmsg[...]), unpacked(kgot[...])
-    both = jnp.concatenate([jnp.where(y == 0, sent, got), jnp.where(y == 0, got, sent)], axis=0).astype(BF)
+    l_sum.step(1)
+
+    for go in k_waits:
+        go.recv()
+    own, other = unpacked(kysend[0]), unpacked(kyrecv[1, 0])
+    for r in range(1, NH):
+        own = own + unpacked(kyrecv[0, r])
+        other = other + unpacked(kyrecv[1, r])
+    unit = by_group(own, other)[:, :E]
+    k_inv = lax.rsqrt(jnp.sum(unit * unit, axis=1, keepdims=True) + EPS)
+    unit = unit * k_inv
+    kunit[...] = unit
+    both = jnp.concatenate([unit, k_ext], axis=1).astype(BF)
 
     def block0(zz, xx):
         return kall.at[rows(64 * zz + 16 * xx, 16), :]
@@ -374,14 +380,7 @@
         for go in first[core]:
             go.start()
 
-    @on_core
-    def _(core):
-        for go in first[core]:
-            go.recv()
-        ring[core].start(0)
-
-
-    l_sum.recv(1)
+    l_sum.end()
     row = l_sum.result()
     l_inv = lax.rsqrt(jnp.sum(row * row, axis=1, keepdims=True) + EPS)
     row = row * l_inv
@@ -391,16 +390,29 @@
 
     @on_core
     def _(core):
-        for s in range(1, ring[core].n // 2):
-            ring[core].recv(s - 1)
-            ring[core].start(s)
+        for go in first[core]:
+            go.recv()
+        ring[core].step(0)
+        ring[core].step(1)
 
     l_spread.step()
+
+    @on_core
+    def _(core):
+        for s in range(2, ring[core].n // 2):
+            ring[core].step(s)
+
     l_spread.last()
 
-    @on_core
-    def _(core):
-        ring[core].recv(ring[core].n // 2 - 1)
+    mine, theirs = kf[...].astype(F32), kfo[...].astype(F32)
+    pieces = []
+    for i in range(2 * NH):
+        pieces.append(by_group(mine[OWN * i : OWN * (i + 1)], theirs[OWN * i : OWN * (i + 1)]))
+    kf2[...] = jnp.concatenate(pieces, axis=0).astype(BF)
+
+    @on_core
+    def _(core):
+        ring[core].end()
 
     l_spread.end()
 
@@ -425,9 +437,7 @@
         @on_core
         def _(core):
             if s < sums[core].n // 2:
-                if s > 0:
-                    sums[core].recv(s - 1)
-                sums[core].start(s)
+                sums[core].step(s)
 
     kpi_side(0, 0)
     step(0)
@@ -450,7 +460,7 @@
 
     g_sum = h_sum(lg, grecv, (grs, grr, gls, glr))
     g_core.recv()
-    g_sum.start(0)
+    g_sum.step(0)
     step(3)
 
     middle = [
@@ -458,14 +468,13 @@
         [Send(lambda r=r: midsend.at[r - 1], lambda r=r: midrecv.at[r - 1], zpeer[r], core=1) for r in ZS],
     ]
 
-    g_sum.recv(0)
-    g_sum.start(1)
+    g_sum.step(1)
 
     @on_core
     def _(core):
         at, order = ((x, XS), (z, ZS))[core]
         n = len(order) + 1
-        sums[core].recv(sums[core].n // 2 - 1)
+        sums[core].end()
         mid[: 16 * n, :] = sums[core].result()
         for r, go in zip(order, middle[core]):
             midsend[r - 1] = mid[rows(16 * mod(at + r, n), 16), :].astype(BF)
@@ -477,30 +486,26 @@
             total = total + midrecv[r].astype(F32)
         mid16[...] = total
 
-    ymsg[...] = packed(mid16[rows(OWN * (1 - y), OWN, OWN), :])
-    y_back = Send(lambda: ymsg, lambda: ygot, other_y)
-    y_back.start()
-    y_back.recv()
-    total = mid16[rows(OWN * y, OWN, OWN), :] + unpacked(ygot[...])[:, :E]
+    total = mid16[...]
     unit = kunit[...]
     inner = jnp.sum(unit * total, axis=1, keepdims=True)
-    kback[c * NH + h] = packed(k_inv * (total - unit * inner))
 
     def kblock(hh):
-        return lambda: kback.at[c * NH + hh]
-
+        return lambda: kback.at[rows(16 * (c * NH + hh), 16), :]
+
+    kback[rows(16 * (c * NH + h), 16), :] = (k_inv * (total - unit * inner)).astype(BF)
     kb_waits = [Send(kblock(h), kblock(h), hpeer[r], kblock(hfrom[r])) for r in (2, 1, 3)]
     for go in kb_waits:
         go.start()
 
-    g_sum.recv(1)
+    g_sum.end()
     row = g_sum.result()
     unit = lunit[...]
     inner = jnp.sum(unit * row, axis=1, keepdims=True)
     row = (l_inv * (row - unit * inner)).astype(BF)
 
     def khalf(core):
-        return lambda: kback.at[pl.ds(core * NH, NH)]
+        return lambda: kback.at[rows(16 * NH * core, 16 * NH), :]
 
     for go in kb_waits:
         go.recv()
@@ -510,8 +515,9 @@
     b_spread.start(row)
     kb_core.recv()
 
-    rows_back = jnp.concatenate([unpacked(kback[i])[:, :E] for i in range(2 * NH)], axis=0).astype(BF)
-    part = lax.dot_general(kf[...], rows_back, (((0,), (0,)), ((), ())), preferred_element_type=F32).astype(BF)
+    part = lax.dot_general(
+        kf2[...], kback[...], (((0,), (0,)), ((), ())), preferred_element_type=F32
+    ).astype(BF)
     tall = part.shape[0]
     for j in range(E // 128):
         wbuf[tall * j : tall * (j + 1), :] = part[:, 128 * j : 128 * (j + 1)]
@@ -532,8 +538,8 @@
         [Send(cut_of(wxs, BLK, mod(z + r, NZ)), slot(wxzr, r - 1), zpeer[r], core=1) for r in ZS],
     ]
     w_pair = [
-        [Send(slot(wy, y), slot(wy, y), other_y, slot(wy, 1 - y), 0)],
-        [Send(slot(wys, y), slot(wys, y), other_y, slot(wys, 1 - y), 1)],
+        [Send(slot(wy, y), slot(wy, y), ypeer[0, 1], slot(wy, 1 - y), 0)],
+        [Send(slot(wys, y), slot(wys, y), ypeer[0, 1], slot(wys, 1 - y), 1)],
     ]
     w_third = [
         [],
@@ -616,44 +622,67 @@
     def _(core):
         arrive(w_last[core])
 
-    for j in range(E // 128):
-        ow[:, 128 * j : 128 * (j + 1)] = wall[tall * j : tall * (j + 1), :].astype(F32)
-    w_out = pltpu.make_async_copy(ow, out_w, lsem.at[7])
+    w_out = pltpu.make_async_copy(wall, out_w, lsem.at[7])
     w_out.start()
     finish()
     g_out.wait()
     w_out.wait()
 
 
+def deliver(g, w, out_g, out_w, wall, ow, sem):
+    first = pltpu.make_async_copy(g, out_g, sem.at[0])
+    second = pltpu.make_async_copy(w, wall, sem.at[1])
+    first.start()
+    second.start()
+    second.wait()
+    tall = out_w.shape[0]
+    for j in range(E // 128):
+        ow[:, 128 * j : 128 * (j + 1)] = wall[tall * j : tall * (j + 1), :].astype(F32)
+    third = pltpu.make_async_copy(ow, out_w, sem.at[2])
+    third.start()
+    first.wait()
+    third.wait()
+
+
 def body(log_feats, kpi_feats, log_proj, kpi_proj, log_ids, kpi_ids):
     v = pltpu.VMEM
-    inputs = (log_feats, kpi_feats, log_proj, kpi_proj, log_ids.reshape(1, -1), kpi_ids.reshape(1, -1))
-    outs = (jax.ShapeDtypeStruct(log_feats.shape, BF), jax.ShapeDtypeStruct(kpi_proj.shape, F32))
-    scratch = [v(a.shape, a.dtype) for a in inputs + outs] + [
+    inputs = (log_feats, kpi_feats, log_proj, kpi_proj, log_ids, kpi_ids.reshape(1, -1))
+    outs = (jax.ShapeDtypeStruct(log_feats.shape, BF), jax.ShapeDtypeStruct((NZ * WZ, 128), BF))
+    hbm = pl.BlockSpec(memory_space=pltpu.HBM)
+    scratch = [v(a.shape, a.dtype) for a in inputs + outs[:1]] + [
         v((HP, E), BF), v((HP, E), BF), v((HP, E), F32), *[v((2, BLK, E), BF)] * 4,
         v((2 * HP, E), BF), v((BLK, E), F32), v((2 * HP, ID), BF),
-        v((GROUP, E), F32), v((32, E), BF), v((32, E), BF), v((3, 16, PK), BF), v((3, 16, PK), BF),
-        v((16, PK), BF), v((16, PK), BF), v((COUNT, EK), BF), v((OWN, E), F32),
+        v((GROUP, E), F32), v((32, E), BF), v((32, E), BF), v((NH, 16, PK), BF), v((2, NH, 16, PK), BF),
+        v(kpi_feats.shape, BF), v((2 * GROUP, kpi_feats.shape[1]), BF), v((1, GROUP), jnp.int32),
+        v((COUNT, EK), BF), v((2 * OWN, E), F32),
         v((2 * HP, COUNT), BF), v((COUNT, E), F32), v((HP, E), F32),
         v((HP, E), BF), v((HP, E), BF), *[v((2, BLK, E), BF)] * 4, v((2 * HP, E), BF),
         *[v((4, 64, E), BF)] * 4, *[v((2, 128, E), BF)] * 4,
-        v((128, E), F32), v((7, 16, E), BF), v((7, 16, E), BF), v((16, E), F32), v((16, PK), BF), v((16, PK), BF),
-        v((2 * NH, 16, PK), BF), v((NZ * WZ, 128), BF), v((NZ - 1, WZ, 128), BF), v((NX - 1, WX, 128), BF),
+        v((128, E), F32), v((7, 16, E), BF), v((7, 16, E), BF), v((16, E), F32),
+        v((2 * NH * 16, E), BF), v((NZ * WZ, 128), BF), v((NZ - 1, WZ, 128), BF), v((NX - 1, WX, 128), BF),
         v((NX, WZ, 128), BF), v((NY, WZ, 128), BF), v((NZ * BLK, 128), BF), v((NZ - 1, BLK, 128), BF),
         v((NY, BLK, 128), BF), v((NZ * BLK, 128), BF), v((NZ * WZ, 128), BF),
         pltpu.SemaphoreType.DMA((NSEM,)), pltpu.SemaphoreType.DMA((NSEM,)),
         pltpu.SemaphoreType.DMA((8,)),
     ]
-    return pl.pallas_call(
+    grads = pl.pallas_call(
         kernel,
         out_shape=outs,
-        in_specs=[pl.BlockSpec(memory_space=pltpu.HBM)] * 6,
-        out_specs=(pl.BlockSpec(memory_space=pltpu.HBM),) * 2,
+        in_specs=[hbm] * 6,
+        out_specs=(hbm,) * 2,
         scratch_shapes=scratch,
         compiler_params=pltpu.CompilerParams(
             collective_id=0, has_side_effects=True, vmem_limit_bytes=62 * 1024 * 1024
         ),
     )(*inputs)
+    return pl.pallas_call(
+        deliver,
+        out_shape=(outs[0], jax.ShapeDtypeStruct(kpi_proj.shape, F32)),
+        in_specs=[hbm] * 2,
+        out_specs=(hbm,) * 2,
+        scratch_shapes=[v(outs[1].shape, BF), v(kpi_proj.shape, F32), pltpu.SemaphoreType.DMA((3,))],
+        compiler_params=pltpu.CompilerParams(vmem_limit_bytes=62 * 1024 * 1024),
+    )(*grads)
 
 
 def solution(mesh):

time: 115 us -> 107 us (0.930); the launches traced: 115 us -> 105 us
  Pallas kernels: 110 us -> 105 us
  local copies, waits for them, and re-layouts: 4.82 us -> 0 us
    pallas_call x1 -> x2, Pallas kernels: 110 us -> 105 us  [the longest x1 98.2 us: body(): pl.pallas_call(kernel, out_shape=outs, in_specs=[hbm] * 6, out_specs=(hbm...]
    unnamed x2 -> x0, local copies, waits for them, and re-layouts: 3.58 us -> none
    reshape x1 -> x0, local copies, waits for them, and re-layouts: 1.25 us -> none  [body(): log_ids.reshape(1, -1)]
where the time goes in v3:
time: 107 us; the launch traced here: 105 us
  Pallas kernels  105 us (98%)
    pallas_call x1, Pallas kernels, body(): pl.pallas_call(kernel, out_shape=outs, in_specs=[hbm] * 6, out_specs=(hbm...  98.2 us
    pallas_call x1, Pallas kernels, body(): pl.pallas_call(deliver, out_shape=(outs[0], jax.ShapeDtypeStruct(kpi_proj...  6.59 us

profile of v3, /device:TPU:1, one launch (start us, length us, event | category | flops | bytes accessed | tf_op | source)
XLA Modules:
  0.0 105.5 jit_solution(15817836067667387775)
XLA Ops:
  0.6 98.2 %shard_map.77 = (bf16[352,256]{1,0:T(8,128)(2,1)}, bf16[1408,128]{1,0:T(8,128)(2,1)}) custom-call(bf16[352,256]{1,0:T(8,128)(2,1)} %lf_h.1, bf16[64,144]{1,0:T(8,128)(2,1)} %kf_h.1, bf16[256,1152]{1,0:T(8,128)(2,1)} %lp_h.1, bf16[144,1152]{1,0:T(8,128)(2,1)} %kp_h.1, s32[352]{0:T(512)} %lid_h.1, s32[1,64]{1,0:T(1,128)} %bitcast.1), custom_call_target="tpu_custom_call" | custom-call | tf_op jit(solution)/shard_map/pallas_call | solution.py:668
  98.9 6.6 %shard_map.78 = (bf16[352,256]{1,0:T(8,128)(2,1)}, f32[144,1152]{1,0:T(8,128)}) custom-call(bf16[352,256]{1,0:T(8,128)(2,1)} %get-tuple-element.4.g, bf16[1408,128]{1,0:T(8,128)(2,1)} %get-tuple-element.5.w), custom_call_target="tpu_custom_call" | custom-call | tf_op jit(solution)/shard_map/pallas_call | solution.py:678

commit v4 on v3

--- a/solution.py
+++ b/solution.py
@@ -72,7 +72,7 @@
     kacc, ksend, krecv, kysend, kyrecv, kfo, kf2, kido, kall, kunit,
     pg, kg, lg, gsend, grecv, grs, grr, gls, glr, back,
     zrs, zrr, zls, zlr, xrs, xrr, xls, xlr, mid, midsend, midrecv, mid16,
-    kback, wbuf, wzr, wxr, wx, wy, wxs, wxzr, wys, wxz, wall,
+    kback, wbuf, wzr, wxr, wx, wy, wxs, wxzr, wys, wxz, wlast,
     ssem, rsem, lsem,
 ):
     d = lax.axis_index("dp")
@@ -285,8 +285,12 @@
     pl.semaphore_wait(barrier, len(peers))
     k_core = Send(lambda: ksend, lambda: krecv, partner)
     k_core.start()
-    l_core = Send(lambda: lsend, lambda: lrecv, partner)
-    l_core.start()
+    l_core = {}
+    for r in (2, 1, 3, 0):
+        out = lambda r=r: lsend.at[rows(BLK * mod(h + r, NH), BLK), :]
+        come = lambda r=r: lrecv.at[rows(BLK * mod(h + r, NH), BLK), :]
+        l_core[r] = Send(out, come, partner)
+        l_core[r].start()
 
     lacc[:HALF, :] = dot(lf[rows(HALF * c, HALF), :], lp[...])
     lacc[HALF:, :] = jnp.zeros((HP - HALF, E), F32)
@@ -308,8 +312,10 @@
                 k_waits.append(go)
 
     l_sum = h_sum(lacc, lrecv, (lrs, lrr, lls, llr))
-    l_core.recv()
+    l_core[2].recv()
     l_sum.step(0)
+    for r in (1, 3, 0):
+        l_core[r].recv()
 
     i_copy.recv()
     f_copy.recv()
@@ -546,9 +552,13 @@
         [Send(cut_of(wxz, BLK, z), cut_of(wxz, BLK, z), zpeer[r], cut_of(wxz, BLK, zfrom[r]), 1) for r in ZS],
     ]
     w_last = [
-        [Send(cut_of(wall, WZ, z), cut_of(wall, WZ, z), zpeer[r], cut_of(wall, WZ, zfrom[r]), 0) for r in ZS],
-        [Send(cut_of(wall, WX, x), cut_of(wall, WX, x), xpeer[r], cut_of(wall, WX, xfrom[r]), 1) for r in XS],
-    ]
+        [Send(slot(wlast, pl.ds(0, WZ)), cut_of(out_w, WZ, z), zpeer[r], cut_of(out_w, WZ, zfrom[r]), 0) for r in ZS],
+        [Send(slot(wlast, pl.ds(0, WX)), cut_of(out_w, WX, x), xpeer[r], cut_of(out_w, WX, xfrom[r]), 1) for r in XS],
+    ]
+
+    def keep(core):
+        size, at = ((WZ, z), (WX, x))[core]
+        return pltpu.make_async_copy(wlast.at[pl.ds(0, size)], cut_of(out_w, size, at)(), lsem.at[7])
 
     def begin(copies):
         for go in copies:
@@ -603,14 +613,14 @@
     def _(core):
         arrive(w_pair[core])
         if core == 0:
-            wall[rows(WZ * z, WZ), :] = (wy[0].astype(F32) + wy[1].astype(F32)).astype(BF)
-            begin(w_last[0])
+            wlast[:WZ, :] = (wy[0].astype(F32) + wy[1].astype(F32)).astype(BF)
         else:
             wxz[rows(BLK * z, BLK), :] = (wys[0].astype(F32) + wys[1].astype(F32)).astype(BF)
             begin(w_third[1])
             arrive(w_third[1])
-            wall[rows(WX * x, WX), :] = wxz[:WX, :]
-            begin(w_last[1])
+            wlast[...] = wxz[:WX, :]
+        begin(w_last[core])
+        keep(core).start()
 
     b_spread.end()
     for i in range(2):
@@ -621,27 +631,28 @@
     @on_core
     def _(core):
         arrive(w_last[core])
-
-    w_out = pltpu.make_async_copy(wall, out_w, lsem.at[7])
-    w_out.start()
+        keep(core).wait()
+
     finish()
     g_out.wait()
-    w_out.wait()
-
-
-def deliver(g, w, out_g, out_w, wall, ow, sem):
-    first = pltpu.make_async_copy(g, out_g, sem.at[0])
-    second = pltpu.make_async_copy(w, wall, sem.at[1])
-    first.start()
-    second.start()
-    second.wait()
+
+
+def deliver(g, w, out_g, out_w, held, wall, ow, sem):
+    copies = [
+        pltpu.make_async_copy(*pair, sem.at[i])
+        for i, pair in enumerate(((w, wall), (g, held), (held, out_g), (ow, out_w)))
+    ]
+    copies[0].start()
+    copies[1].start()
+    copies[1].wait()
+    copies[2].start()
+    copies[0].wait()
     tall = out_w.shape[0]
     for j in range(E // 128):
         ow[:, 128 * j : 128 * (j + 1)] = wall[tall * j : tall * (j + 1), :].astype(F32)
-    third = pltpu.make_async_copy(ow, out_w, sem.at[2])
-    third.start()
-    first.wait()
-    third.wait()
+    copies[3].start()
+    copies[2].wait()
+    copies[3].wait()
 
 
 def body(log_feats, kpi_feats, log_proj, kpi_proj, log_ids, kpi_ids):
@@ -661,7 +672,7 @@
         v((128, E), F32), v((7, 16, E), BF), v((7, 16, E), BF), v((16, E), F32),
         v((2 * NH * 16, E), BF), v((NZ * WZ, 128), BF), v((NZ - 1, WZ, 128), BF), v((NX - 1, WX, 128), BF),
         v((NX, WZ, 128), BF), v((NY, WZ, 128), BF), v((NZ * BLK, 128), BF), v((NZ - 1, BLK, 128), BF),
-        v((NY, BLK, 128), BF), v((NZ * BLK, 128), BF), v((NZ * WZ, 128), BF),
+        v((NY, BLK, 128), BF), v((NZ * BLK, 128), BF), v((WX, 128), BF),
         pltpu.SemaphoreType.DMA((NSEM,)), pltpu.SemaphoreType.DMA((NSEM,)),
         pltpu.SemaphoreType.DMA((8,)),
     ]
@@ -680,7 +691,7 @@
         out_shape=(outs[0], jax.ShapeDtypeStruct(kpi_proj.shape, F32)),
         in_specs=[hbm] * 2,
         out_specs=(hbm,) * 2,
-        scratch_shapes=[v(outs[1].shape, BF), v(kpi_proj.shape, F32), pltpu.SemaphoreType.DMA((3,))],
+        scratch_shapes=[v(outs[0].shape, BF), v(outs[1].shape, BF), v(kpi_proj.shape, F32), pltpu.SemaphoreType.DMA((4,))],
         compiler_params=pltpu.CompilerParams(vmem_limit_bytes=62 * 1024 * 1024),
     )(*grads)
 

time: 107 us -> 101 us (0.944)
  Pallas kernels: 105 us -> 99.8 us
    pallas_call x1, Pallas kernels: 6.59 us -> 1.96 us  [body(): pl.pallas_call(deliver, out_shape=(outs[0], jax.ShapeDtypeStruct(kpi_proj...]
where the time goes in v4:
time: 101 us; the launch traced here: 100 us
  Pallas kernels  99.8 us (99%)
    pallas_call x1, Pallas kernels, body(): pl.pallas_call(kernel, out_shape=outs, in_specs=[hbm] * 6, out_specs=(hbm...  97.8 us

profile of v4, /device:TPU:1, one launch (start us, length us, event | category | flops | bytes accessed | tf_op | source)
XLA Modules:
  0.0 100.4 jit_solution(9441287965271101693)
XLA Ops:
  0.6 97.8 %shard_map.77 = (bf16[352,256]{1,0:T(8,128)(2,1)}, bf16[1408,128]{1,0:T(8,128)(2,1)}) custom-call(bf16[352,256]{1,0:T(8,128)(2,1)} %lf_h.1, bf16[64,144]{1,0:T(8,128)(2,1)} %kf_h.1, bf16[256,1152]{1,0:T(8,128)(2,1)} %lp_h.1, bf16[144,1152]{1,0:T(8,128)(2,1)} %kp_h.1, s32[352]{0:T(512)} %lid_h.1, s32[1,64]{1,0:T(1,128)} %bitcast.1), custom_call_target="tpu_custom_call" | custom-call | tf_op jit(solution)/shard_map/pallas_call | solution.py:679
  98.5 2.0 %shard_map.78 = (bf16[352,256]{1,0:T(8,128)(2,1)}, f32[144,1152]{1,0:T(8,128)}) custom-call(bf16[352,256]{1,0:T(8,128)(2,1)} %get-tuple-element.4.g, bf16[1408,128]{1,0:T(8,128)(2,1)} %get-tuple-element.5.w), custom_call_target="tpu_custom_call" | custom-call | tf_op jit(solution)/shard_map/pallas_call | solution.py:689

commit v5 on v4

--- a/solution.py
+++ b/solution.py
@@ -458,23 +458,21 @@
         return carry
 
     lax.fori_loop(0, COUNT // 256, log_pairs, 0)
+    step(2)
     gsend[...] = dot(pg[rows(HP * (1 - c), HP), :], kall[:, :E]).astype(BF)
     g_core = Send(lambda: gsend, lambda: grecv, partner)
     g_core.start()
-    step(2)
     lg[...] = dot(pg[rows(HP * c, HP), :], kall[:, :E])
 
     g_sum = h_sum(lg, grecv, (grs, grr, gls, glr))
+    step(3)
     g_core.recv()
     g_sum.step(0)
-    step(3)
 
     middle = [
         [Send(lambda r=r: midsend.at[r - 1], lambda r=r: midrecv.at[r - 1], xpeer[r], core=0) for r in XS],
         [Send(lambda r=r: midsend.at[r - 1], lambda r=r: midrecv.at[r - 1], zpeer[r], core=1) for r in ZS],
     ]
-
-    g_sum.step(1)
 
     @on_core
     def _(core):
@@ -485,6 +483,13 @@
         for r, go in zip(order, middle[core]):
             midsend[r - 1] = mid[rows(16 * mod(at + r, n), 16), :].astype(BF)
             go.start()
+
+    g_sum.step(1)
+
+    @on_core
+    def _(core):
+        at, order = ((x, XS), (z, ZS))[core]
+        n = len(order) + 1
         total = mid[rows(16 * at, 16), :]
         for go in middle[core]:
             go.recv()
@@ -496,13 +501,17 @@
     unit = kunit[...]
     inner = jnp.sum(unit * total, axis=1, keepdims=True)
 
-    def kblock(hh):
-        return lambda: kback.at[rows(16 * (c * NH + hh), 16), :]
+    def kblock(core, hh):
+        return lambda: kback.at[rows(16 * (core * NH + hh), 16), :]
 
     kback[rows(16 * (c * NH + h), 16), :] = (k_inv * (total - unit * inner)).astype(BF)
-    kb_waits = [Send(kblock(h), kblock(h), hpeer[r], kblock(hfrom[r])) for r in (2, 1, 3)]
-    for go in kb_waits:
+    kb_waits = {r: Send(kblock(c, h), kblock(c, h), hpeer[r], kblock(c, hfrom[r])) for r in (2, 1, 3)}
+    for go in kb_waits.values():
         go.start()
+    kb_core = {
+        r: Send(kblock(c, hfrom[r]), kblock(c, hfrom[r]), partner, kblock(1 - c, hfrom[r])) for r in range(NH)
+    }
+    kb_core[0].start()
 
     g_sum.end()
     row = g_sum.result()
@@ -510,16 +519,13 @@
     inner = jnp.sum(unit * row, axis=1, keepdims=True)
     row = (l_inv * (row - unit * inner)).astype(BF)
 
-    def khalf(core):
-        return lambda: kback.at[rows(16 * NH * core, 16 * NH), :]
-
-    for go in kb_waits:
-        go.recv()
-    kb_core = Send(khalf(c), khalf(c), partner, khalf(1 - c))
-    kb_core.start()
+    for r in (1, 3, 2):
+        kb_waits[r].recv()
+        kb_core[r].start()
     b_spread = Spread(back)
     b_spread.start(row)
-    kb_core.recv()
+    for r in (0, 1, 3, 2):
+        kb_core[r].recv()
 
     part = lax.dot_general(
         kf2[...], kback[...], (((0,), (0,)), ((), ())), preferred_element_type=F32

time: 101 us -> 101 us (level)
  Pallas kernels: 99.8 us -> 101 us
where the time goes in v5:
time: 101 us
  Pallas kernels  101 us (100%)
    pallas_call x1, Pallas kernels, body(): pl.pallas_call(kernel, out_shape=outs, in_specs=[hbm] * 6, out_specs=(hbm...  98.6 us

profile of v5, /device:TPU:1, one launch (start us, length us, event | category | flops | bytes accessed | tf_op | source)
XLA Modules:
  0.0 101.2 jit_solution(2290458847711745005)
XLA Ops:
  0.6 98.6 %shard_map.77 = (bf16[352,256]{1,0:T(8,128)(2,1)}, bf16[1408,128]{1,0:T(8,128)(2,1)}) custom-call(bf16[352,256]{1,0:T(8,128)(2,1)} %lf_h.1, bf16[64,144]{1,0:T(8,128)(2,1)} %kf_h.1, bf16[256,1152]{1,0:T(8,128)(2,1)} %lp_h.1, bf16[144,1152]{1,0:T(8,128)(2,1)} %kp_h.1, s32[352]{0:T(512)} %lid_h.1, s32[1,64]{1,0:T(1,128)} %bitcast.1), custom_call_target="tpu_custom_call" | custom-call | tf_op jit(solution)/shard_map/pallas_call | solution.py:685
  99.2 2.0 %shard_map.78 = (bf16[352,256]{1,0:T(8,128)(2,1)}, f32[144,1152]{1,0:T(8,128)}) custom-call(bf16[352,256]{1,0:T(8,128)(2,1)} %get-tuple-element.4.g, bf16[1408,128]{1,0:T(8,128)(2,1)} %get-tuple-element.5.w), custom_call_target="tpu_custom_call" | custom-call | tf_op jit(solution)/shard_map/pallas_call | solution.py:695

commit v6 on v5

--- a/solution.py
+++ b/solution.py
@@ -457,25 +457,16 @@
         pg[:, at] = pair_gradient(inner, apart)
         return carry
 
-    lax.fori_loop(0, COUNT // 256, log_pairs, 0)
+    log_pairs(0, 0)
     step(2)
-    gsend[...] = dot(pg[rows(HP * (1 - c), HP), :], kall[:, :E]).astype(BF)
-    g_core = Send(lambda: gsend, lambda: grecv, partner)
-    g_core.start()
-    lg[...] = dot(pg[rows(HP * c, HP), :], kall[:, :E])
-
-    g_sum = h_sum(lg, grecv, (grs, grr, gls, glr))
+    log_pairs(1, 0)
     step(3)
-    g_core.recv()
-    g_sum.step(0)
-
     middle = [
         [Send(lambda r=r: midsend.at[r - 1], lambda r=r: midrecv.at[r - 1], xpeer[r], core=0) for r in XS],
         [Send(lambda r=r: midsend.at[r - 1], lambda r=r: midrecv.at[r - 1], zpeer[r], core=1) for r in ZS],
     ]
 
-    @on_core
-    def _(core):
+    def middle_begin(core):
         at, order = ((x, XS), (z, ZS))[core]
         n = len(order) + 1
         sums[core].end()
@@ -484,7 +475,16 @@
             midsend[r - 1] = mid[rows(16 * mod(at + r, n), 16), :].astype(BF)
             go.start()
 
-    g_sum.step(1)
+    pl.when(c == 1)(lambda: middle_begin(1))
+    gsend[...] = dot(pg[rows(HP * (1 - c), HP), :], kall[:, :E]).astype(BF)
+    g_core = Send(lambda: gsend, lambda: grecv, partner)
+    g_core.start()
+
+    pl.when(c == 0)(lambda: middle_begin(0))
+    lg[...] = dot(pg[rows(HP * c, HP), :], kall[:, :E])
+    g_sum = h_sum(lg, grecv, (grs, grr, gls, glr))
+    g_core.recv()
+    g_sum.step(0)
 
     @on_core
     def _(core):
@@ -513,17 +513,10 @@
     }
     kb_core[0].start()
 
-    g_sum.end()
-    row = g_sum.result()
-    unit = lunit[...]
-    inner = jnp.sum(unit * row, axis=1, keepdims=True)
-    row = (l_inv * (row - unit * inner)).astype(BF)
-
+    g_sum.step(1)
     for r in (1, 3, 2):
         kb_waits[r].recv()
         kb_core[r].start()
-    b_spread = Spread(back)
-    b_spread.start(row)
     for r in (0, 1, 3, 2):
         kb_core[r].recv()
 
@@ -578,7 +571,13 @@
     def _(core):
         begin(w_first[core])
 
-    b_spread.step()
+    g_sum.end()
+    row = g_sum.result()
+    unit = lunit[...]
+    inner = jnp.sum(unit * row, axis=1, keepdims=True)
+    row = (l_inv * (row - unit * inner)).astype(BF)
+    b_spread = Spread(back)
+    b_spread.start(row)
 
     @on_core
     def _(core):
@@ -597,7 +596,7 @@
             wxs[WX:, :] = jnp.zeros((NZ * BLK - WX, 128), BF)
         begin(w_second[core])
 
-    b_spread.last()
+    b_spread.step()
 
     @on_core
     def _(core):
@@ -628,6 +627,7 @@
         begin(w_last[core])
         keep(core).start()
 
+    b_spread.last()
     b_spread.end()
     for i in range(2):
         og[HALF * i : HALF * (i + 1), :] = dot_t(back[HP * i : HP * i + HALF, :], lp[...]).astype(BF)

time: 101 us -> 102 us (level)
  no operation moved by 1% of the time
where the time goes in v6:
time: 102 us
  Pallas kernels  101 us (99%)
    pallas_call x1, Pallas kernels, body(): pl.pallas_call(kernel, out_shape=outs, in_specs=[hbm] * 6, out_specs=(hbm...  98.9 us

profile of v6, /device:TPU:1, one launch (start us, length us, event | category | flops | bytes accessed | tf_op | source)
XLA Modules:
  0.0 101.5 jit_solution(17409592062715708723)
XLA Ops:
  0.6 98.9 %shard_map.77 = (bf16[352,256]{1,0:T(8,128)(2,1)}, bf16[1408,128]{1,0:T(8,128)(2,1)}) custom-call(bf16[352,256]{1,0:T(8,128)(2,1)} %lf_h.1, bf16[64,144]{1,0:T(8,128)(2,1)} %kf_h.1, bf16[256,1152]{1,0:T(8,128)(2,1)} %lp_h.1, bf16[144,1152]{1,0:T(8,128)(2,1)} %kp_h.1, s32[352]{0:T(512)} %lid_h.1, s32[1,64]{1,0:T(1,128)} %bitcast.1), custom_call_target="tpu_custom_call" | custom-call | tf_op jit(solution)/shard_map/pallas_call | solution.py:685
  99.6 2.0 %shard_map.78 = (bf16[352,256]{1,0:T(8,128)(2,1)}, f32[144,1152]{1,0:T(8,128)}) custom-call(bf16[352,256]{1,0:T(8,128)(2,1)} %get-tuple-element.4.g, bf16[1408,128]{1,0:T(8,128)(2,1)} %get-tuple-element.5.w), custom_call_target="tpu_custom_call" | custom-call | tf_op jit(solution)/shard_map/pallas_call | solution.py:695

commit v7 on v5

--- a/solution.py
+++ b/solution.py
@@ -134,7 +134,7 @@
 
     inputs = [
         pltpu.make_async_copy(a, b, lsem.at[i])
-        for i, (a, b) in enumerate(((kf_h, kf), (kp_h, kp), (lf_h, lf), (lp_h, lp), (kid_h, kid), (lid_h, lid)))
+        for i, (a, b) in enumerate(((lf_h, lf), (lp_h, lp), (kf_h, kf), (kp_h, kp), (kid_h, kid), (lid_h, lid)))
     ]
     for go in inputs:
         go.start()
@@ -273,24 +273,22 @@
 
     inputs[0].wait()
     inputs[1].wait()
-    kacc[...] = dot(kf[...], kp[...])
-    ksend[...] = kacc[rows(32 * (1 - c), 32, 32), :].astype(BF)
-    inputs[2].wait()
-    inputs[3].wait()
     lsend[:HALF, :] = dot(lf[rows(HALF * (1 - c), HALF), :], lp[...]).astype(BF)
     lsend[HALF:, :] = jnp.zeros((HP - HALF, E), BF)
-    inputs[4].wait()
-    inputs[5].wait()
+    for go in inputs[2:]:
+        go.wait()
 
     pl.semaphore_wait(barrier, len(peers))
-    k_core = Send(lambda: ksend, lambda: krecv, partner)
-    k_core.start()
     l_core = {}
     for r in (2, 1, 3, 0):
         out = lambda r=r: lsend.at[rows(BLK * mod(h + r, NH), BLK), :]
         come = lambda r=r: lrecv.at[rows(BLK * mod(h + r, NH), BLK), :]
         l_core[r] = Send(out, come, partner)
         l_core[r].start()
+    kacc[...] = dot(kf[...], kp[...])
+    ksend[...] = kacc[rows(32 * (1 - c), 32, 32), :].astype(BF)
+    k_core = Send(lambda: ksend, lambda: krecv, partner)
+    k_core.start()
 
     lacc[:HALF, :] = dot(lf[rows(HALF * c, HALF), :], lp[...])
     lacc[HALF:, :] = jnp.zeros((HP - HALF, E), F32)
@@ -299,6 +297,12 @@
     f_copy.start()
     i_copy = Send(lambda: kid, lambda: kido, ypeer[0, 1])
     i_copy.start()
+
+    l_sum = h_sum(lacc, lrecv, (lrs, lrr, lls, llr))
+    l_core[2].recv()
+    l_sum.step(0)
+    for r in (1, 3, 0):
+        l_core[r].recv()
 
     k_core.recv()
     kacc[rows(32 * c, 32, 32), :] += krecv[...].astype(F32)
@@ -310,12 +314,6 @@
                 go = Send(lambda r=r: kysend.at[r], lambda r=r, f=f: kyrecv.at[f, r], ypeer[r, f])
                 go.start()
                 k_waits.append(go)
-
-    l_sum = h_sum(lacc, lrecv, (lrs, lrr, lls, llr))
-    l_core[2].recv()
-    l_sum.step(0)
-    for r in (1, 3, 0):
-        l_core[r].recv()
 
     i_copy.recv()
     f_copy.recv()

time: 101 us -> 101 us (level)
  Pallas kernels: 101 us -> 99.9 us
where the time goes in v7:
time: 101 us
  Pallas kernels  99.9 us (99%)
    pallas_call x1, Pallas kernels, body(): pl.pallas_call(kernel, out_shape=outs, in_specs=[hbm] * 6, out_specs=(hbm...  97.9 us

profile of v7, /device:TPU:1, one launch (start us, length us, event | category | flops | bytes accessed | tf_op | source)
XLA Modules:
  0.0 100.5 jit_solution(15503158564206216412)
XLA Ops:
  0.6 97.9 %shard_map.77 = (bf16[352,256]{1,0:T(8,128)(2,1)}, bf16[1408,128]{1,0:T(8,128)(2,1)}) custom-call(bf16[352,256]{1,0:T(8,128)(2,1)} %lf_h.1, bf16[64,144]{1,0:T(8,128)(2,1)} %kf_h.1, bf16[256,1152]{1,0:T(8,128)(2,1)} %lp_h.1, bf16[144,1152]{1,0:T(8,128)(2,1)} %kp_h.1, s32[352]{0:T(512)} %lid_h.1, s32[1,64]{1,0:T(1,128)} %bitcast.1), custom_call_target="tpu_custom_call" | custom-call | tf_op jit(solution)/shard_map/pallas_call | solution.py:683
  98.6 2.0 %shard_map.78 = (bf16[352,256]{1,0:T(8,128)(2,1)}, f32[144,1152]{1,0:T(8,128)}) custom-call(bf16[352,256]{1,0:T(8,128)(2,1)} %get-tuple-element.4.g, bf16[1408,128]{1,0:T(8,128)(2,1)} %get-tuple-element.5.w), custom_call_target="tpu_custom_call" | custom-call | tf_op jit(solution)/shard_map/pallas_call | solution.py:693

commit v8 on v7

--- a/solution.py
+++ b/solution.py
@@ -576,8 +576,6 @@
     def _(core):
         begin(w_first[core])
 
-    b_spread.step()
-
     @on_core
     def _(core):
         if core == 0:
@@ -595,7 +593,7 @@
             wxs[WX:, :] = jnp.zeros((NZ * BLK - WX, 128), BF)
         begin(w_second[core])
 
-    b_spread.last()
+    b_spread.step()
 
     @on_core
     def _(core):
@@ -626,6 +624,7 @@
         begin(w_last[core])
         keep(core).start()
 
+    b_spread.last()
     b_spread.end()
     for i in range(2):
         og[HALF * i : HALF * (i + 1), :] = dot_t(back[HP * i : HP * i + HALF, :], lp[...]).astype(BF)

time: 101 us -> 101 us (level)
  no operation moved by 1% of the time
where the time goes in v8:
time: 101 us; the launch traced here: 100 us
  Pallas kernels  99.7 us (99%)
    pallas_call x1, Pallas kernels, body(): pl.pallas_call(kernel, out_shape=outs, in_specs=[hbm] * 6, out_specs=(hbm...  97.8 us

profile of v8, /device:TPU:1, one launch (start us, length us, event | category | flops | bytes accessed | tf_op | source)
XLA Modules:
  0.0 100.4 jit_solution(13954042889797582402)
XLA Ops:
  0.6 97.8 %shard_map.77 = (bf16[352,256]{1,0:T(8,128)(2,1)}, bf16[1408,128]{1,0:T(8,128)(2,1)}) custom-call(bf16[352,256]{1,0:T(8,128)(2,1)} %lf_h.1, bf16[64,144]{1,0:T(8,128)(2,1)} %kf_h.1, bf16[256,1152]{1,0:T(8,128)(2,1)} %lp_h.1, bf16[144,1152]{1,0:T(8,128)(2,1)} %kp_h.1, s32[352]{0:T(512)} %lid_h.1, s32[1,64]{1,0:T(1,128)} %bitcast.1), custom_call_target="tpu_custom_call" | custom-call | tf_op jit(solution)/shard_map/pallas_call | solution.py:682
  98.4 2.0 %shard_map.78 = (bf16[352,256]{1,0:T(8,128)(2,1)}, f32[144,1152]{1,0:T(8,128)}) custom-call(bf16[352,256]{1,0:T(8,128)(2,1)} %get-tuple-element.4.g, bf16[1408,128]{1,0:T(8,128)(2,1)} %get-tuple-element.5.w), custom_call_target="tpu_custom_call" | custom-call | tf_op jit(solution)/shard_map/pallas_call | solution.py:692
